TPU v7x, 256 devices: a whole 4x4x8 slice. The times are simulated.
256 devices in a mesh: region: 32 (over y, z), group: 8 (over x, core).
Axes of the slice: x: 4, y: 4, z: 8, core: 2. Of those that a mesh axis runs over, the one named last changes fastest.
Arguments:
- points: bfloat16 [8, 8192, 512], P('group', 'region'), may hold values from -60 to 60
- row_slot: int32 [8, 8192], P('group', 'region'), may hold values from 0 to 511, as said below
- pos_slot: int32 [8, 8192], P('group', 'region'), may hold values from 0 to 511, as said below
- patch_ids: int32 [8, 32, 256], P('group', 'region'), may hold values from 0 to 3, as said below
- bn_gain: float32 [512], replicated, may hold values from 0.1 to 1.9
- bn_bias: float32 [512], replicated, may hold values from -3 to 3
- w_qkv: bfloat16 [512, 1536], replicated, may hold values from -0.25 to 0.25
- w_proj: bfloat16 [512, 512], replicated, may hold values from -1.5 to 1.5
- cotangent: bfloat16 [8, 8192, 512], P('group', 'region'), may hold values from -2 to 2
Outputs:
- output: bfloat16 [8, 8192, 512], P('group', 'region')
- grad_points: bfloat16 [8, 8192, 512], P('group', 'region')
- grad_w_qkv: float32 [512, 1536], P('group', 'region')
- grad_w_proj: float32 [512, 512], P('group', 'region')
- grad_gain: float32 [512], replicated
- grad_bias: float32 [512], replicated
Inputs may be any that keep to these rules, and one draw needn't show every extreme that they name: Values of one device's 256 points are distinct; row_slot // 16 is the destination range and row_slot % 16 the slot within it. Each device sends at most 16 points to one range, and in every window some device sends exactly 16 to some range. Values of one range's 256 positions are distinct; pos_slot // 16 is the source brick and pos_slot % 16 the slot it used, so row_slot and pos_slot describe one bijection between brick and serialized positions of a window, and every range receives exactly 256 points. `patch_ids`: ids count patches within one device's range of 256 serialized positions, never falling along it; a patch never leaves that range and holds at most 256 positions, and in every window some patch holds exactly 256.
All inputs are finite; a program needn't handle non-finite values.
Results may differ from a plain program's by a relative error of at most 0.025.
Values may be sent and summed in bfloat16 or wider, within the bound.
A program may use at most 64 MiB of HBM per device.

v0:
```python
import jax
import jax.numpy as jnp
from jax import lax
from jax.sharding import PartitionSpec as P

HEAD_DIM = 16


EPS = 1e-05


def masked_softmax(scores, in_patch):
    scores = jnp.where(in_patch[None], scores, -1e30)
    highest = jnp.max(scores, axis=-1, keepdims=True)
    raised = jnp.exp(scores - highest)
    return raised / jnp.sum(raised, axis=-1, keepdims=True)


def head_block(source, row_start, row_count, first_col, col_span):
    return source[row_start : row_start + row_count, first_col : first_col + col_span].reshape(
        row_count, col_span // HEAD_DIM, HEAD_DIM
    )


def attend_forward(qkv_rows, patch_row):
    row_count = qkv_rows.shape[0]
    channels = qkv_rows.shape[1] // 3
    col_span = min(128, channels)
    row_block = min(512, row_count)
    factor = HEAD_DIM ** (-0.5)
    columns = []
    for first_col in range(0, channels, col_span):
        key_heads = head_block(qkv_rows, 0, row_count, channels + first_col, col_span)
        value_heads = head_block(qkv_rows, 0, row_count, 2 * channels + first_col, col_span)
        query_heads = head_block(qkv_rows, 0, row_block, first_col, col_span)
        in_patch = patch_row[0:row_block, None] == patch_row[None, :]
        scores = (
            jnp.einsum("qhd,khd->hqk", query_heads, key_heads, preferred_element_type=jnp.float32)
            * factor
        )
        weights = masked_softmax(scores, in_patch).astype(jnp.bfloat16)
        mixed = jnp.einsum("hqk,khd->qhd", weights, value_heads, preferred_element_type=jnp.float32)
        pieces = mixed.reshape(row_block, col_span).astype(jnp.bfloat16)
        columns.append(pieces)
    return jnp.concatenate(columns, axis=1)


def attend_backward(qkv_rows, patch_row, grad_mixed):
    row_count = qkv_rows.shape[0]
    channels = qkv_rows.shape[1] // 3
    col_span = min(128, channels)
    row_block = min(512, row_count)
    factor = HEAD_DIM ** (-0.5)
    query_cols = []
    key_cols = []
    value_cols = []
    for first_col in range(0, channels, col_span):
        key_heads = head_block(qkv_rows, 0, row_count, channels + first_col, col_span)
        value_heads = head_block(qkv_rows, 0, row_count, 2 * channels + first_col, col_span)
        query_heads = head_block(qkv_rows, 0, row_block, first_col, col_span)
        grad_heads = head_block(grad_mixed, 0, row_block, first_col, col_span)
        in_patch = patch_row[0:row_block, None] == patch_row[None, :]
        scores = (
            jnp.einsum("qhd,khd->hqk", query_heads, key_heads, preferred_element_type=jnp.float32)
            * factor
        )
        probs = masked_softmax(scores, in_patch)
        weights = probs.astype(jnp.bfloat16)
        grad_weights = jnp.einsum(
            "qhd,khd->hqk", grad_heads, value_heads, preferred_element_type=jnp.float32
        )
        value_grad = jnp.einsum(
            "hqk,qhd->khd", weights, grad_heads, preferred_element_type=jnp.float32
        )
        grad_scores = probs * (grad_weights - jnp.sum(probs * grad_weights, axis=-1, keepdims=True))
        grad_scores = grad_scores.astype(jnp.bfloat16)
        query_grad = (
            jnp.einsum("hqk,khd->qhd", grad_scores, key_heads, preferred_element_type=jnp.float32)
            * factor
        )
        query_parts = query_grad.reshape(row_block, col_span).astype(jnp.bfloat16)
        key_grad = jnp.einsum(
            "hqk,qhd->khd", grad_scores, query_heads, preferred_element_type=jnp.float32
        )
        query_cols.append(query_parts)
        key_cols.append((key_grad * factor).reshape(row_count, col_span).astype(jnp.bfloat16))
        value_cols.append(value_grad.reshape(row_count, col_span).astype(jnp.bfloat16))
    return jnp.concatenate(query_cols + key_cols + value_cols, axis=1)


def to_slots(rows_in, slot_index, region_size, capacity):
    filled = (
        jnp.zeros((region_size * capacity, rows_in.shape[1]), rows_in.dtype)
        .at[slot_index]
        .set(rows_in)
    )
    return filled.reshape(region_size, capacity, rows_in.shape[1])


def from_slots(arrived, slot_index):
    return arrived.reshape(arrived.shape[0] * arrived.shape[1], arrived.shape[2])[slot_index]


def on_device(points, row_slot, pos_slot, patch_ids, bn_gain, bn_bias, w_qkv, w_proj, cotangent):
    region_size = lax.axis_size("region")
    point_count = points.shape[1]
    capacity = 2 * point_count // region_size
    count_all = point_count * region_size * lax.axis_size("group")
    local_rows = points[0].astype(jnp.float32)
    send_rows = row_slot[0]
    recv_rows = pos_slot[0]
    patch_row = patch_ids[0, 0]
    mean_all = lax.psum(jnp.sum(local_rows, axis=0), ("region", "group")) / count_all
    centered = local_rows - mean_all
    spread = lax.psum(jnp.sum(centered * centered, axis=0), ("region", "group")) / count_all
    inv_std = lax.rsqrt(spread + EPS)
    unit_rows = centered * inv_std
    normed = (unit_rows * bn_gain + bn_bias).astype(jnp.bfloat16)
    arrived = lax.all_to_all(
        to_slots(normed, send_rows, region_size, capacity),
        "region",
        split_axis=0,
        concat_axis=0,
        tiled=True,
    )
    serial = from_slots(arrived, recv_rows)
    qkv_rows = jnp.dot(serial, w_qkv, preferred_element_type=jnp.float32).astype(jnp.bfloat16)
    mixed = attend_forward(qkv_rows, patch_row)
    grad_home_rows = cotangent[0]
    branch = jnp.dot(mixed, w_proj, preferred_element_type=jnp.float32).astype(jnp.bfloat16)
    returned = lax.all_to_all(
        to_slots(branch, recv_rows, region_size, capacity),
        "region",
        split_axis=0,
        concat_axis=0,
        tiled=True,
    )
    output = from_slots(returned, send_rows)
    sent_grad = lax.all_to_all(
        to_slots(grad_home_rows, send_rows, region_size, capacity),
        "region",
        split_axis=0,
        concat_axis=0,
        tiled=True,
    )
    grad_serial = from_slots(sent_grad, recv_rows)
    proj_grad = jnp.einsum("pc,pd->cd", mixed, grad_serial, preferred_element_type=jnp.float32)
    grad_mixed = jnp.einsum(
        "pd,cd->pc", grad_serial, w_proj, preferred_element_type=jnp.float32
    ).astype(jnp.bfloat16)
    grad_qkv = attend_backward(qkv_rows, patch_row, grad_mixed)
    qkv_grad = jnp.einsum("pc,pd->cd", serial, grad_qkv, preferred_element_type=jnp.float32)
    grad_serial_in = jnp.einsum(
        "pd,cd->pc", grad_qkv, w_qkv, preferred_element_type=jnp.float32
    ).astype(jnp.bfloat16)
    came_home = lax.all_to_all(
        to_slots(grad_serial_in, recv_rows, region_size, capacity),
        "region",
        split_axis=0,
        concat_axis=0,
        tiled=True,
    )
    grad_normed = from_slots(came_home, send_rows).astype(jnp.float32)
    grad_bias, grad_gain = lax.psum(
        (jnp.sum(grad_normed, axis=0), jnp.sum(grad_normed * unit_rows, axis=0)),
        ("region", "group"),
    )
    grad_points = inv_std * (
        grad_normed * bn_gain
        - bn_gain * grad_bias / count_all
        - unit_rows * (bn_gain * grad_gain / count_all)
    )
    qkv_rows_part, proj_rows_part = (
        lax.psum_scatter(
            qkv_grad.astype(jnp.bfloat16), "group", scatter_dimension=0, tiled=True
        ).astype(jnp.float32),
        lax.psum_scatter(
            proj_grad.astype(jnp.bfloat16), "group", scatter_dimension=0, tiled=True
        ).astype(jnp.float32),
    )
    qkv_share, proj_share = (
        lax.psum_scatter(
            qkv_rows_part.astype(jnp.bfloat16), "region", scatter_dimension=1, tiled=True
        ).astype(jnp.float32),
        lax.psum_scatter(
            proj_rows_part.astype(jnp.bfloat16), "region", scatter_dimension=1, tiled=True
        ).astype(jnp.float32),
    )
    return (
        output[None],
        grad_points.astype(jnp.bfloat16)[None],
        qkv_share,
        proj_share,
        grad_gain,
        grad_bias,
    )


def solution(mesh):
    placed = (
        P("group", "region", None),
        P("group", "region"),
        P("group", "region"),
        P("group", "region", None),
        P(),
        P(),
        P(),
        P(),
        P("group", "region", None),
    )
    return jax.shard_map(
        on_device,
        mesh=mesh,
        in_specs=placed,
        out_specs=(
            P("group", "region", None),
            P("group", "region", None),
            P("group", "region"),
            P("group", "region"),
            P(),
            P(),
        ),
        check_vma=False,
    )
```

profile of v0, /device:TPU:1, one launch (start us, length us, event | category | flops | bytes accessed | tf_op | source)
XLA Modules:
  0.0 719.0 jit_solution(6339550225530371514)
XLA Ops:
  8.0 1.0 convert_reduce_fusion.1
  9.1 81.4 %psum.28 = f32[512]{0:T(512)S(1)} all-reduce(f32[512]{0:T(512)S(1)} %convert_reduce_fusion.1), channel_id=1, replica_groups=mesh['region'=32,'group'=8] {'region','group'}, use_global_device_ids=true, to_apply=%region_1.0 | all-reduce | flops 512 | bytes 4096 | tf_op jit(solution)/shard_map/psum | solution.py:113
  90.5 1.0 fusion.34
  91.5 72.4 %psum.29 = f32[512]{0:T(512)S(1)} all-reduce(f32[512]{0:T(512)S(1)} %fusion.34), channel_id=1, replica_groups=mesh['region'=32,'group'=8] {'region','group'}, use_global_device_ids=true, to_apply=%region_3.0 | all-reduce | flops 512 | bytes 4096 | tf_op jit(solution)/shard_map/psum | solution.py:115
  163.9 2.8 scatter_custom_fusion
  166.7 6.1 all-to-all-start
  172.8 2.3 scatter_custom_fusion.2
  175.1 12.0 %all-to-all-done = bf16[32,16,512]{2,1,0:T(8,128)(2,1)S(1)} async-done(((bf16[32,16,512]{2,1,0:T(8,128)(2,1)}), bf16[32,16,512]{2,1,0:T(8,128)(2,1)S(1)}, u32[]{:S(2)}, u32[]{:S(2)}) %all-to-all-start) | async-done | bytes 524320 | tf_op jit(solution)/shard_map/all_to_all | solution.py:119
  187.1 7.5 %all-to-all-start.2 = ((bf16[32,16,512]{2,1,0:T(8,128)(2,1)}), bf16[32,16,512]{2,1,0:T(8,128)(2,1)S(1)}, u32[]{:S(2)}, u32[]{:S(2)}) async-start(bf16[32,16,512]{2,1,0:T(8,128)(2,1)} %bitcast.32), calls=%async_computation.2 | async-start | bytes 1048576 | tf_op jit(solution)/shard_map/all_to_all | solution.py:139
  195.0 1.2 gather_fusion
  196.1 12.0 %all-to-all-done.2 = bf16[32,16,512]{2,1,0:T(8,128)(2,1)S(1)} async-done(((bf16[32,16,512]{2,1,0:T(8,128)(2,1)}), bf16[32,16,512]{2,1,0:T(8,128)(2,1)S(1)}, u32[]{:S(2)}, u32[]{:S(2)}) %all-to-all-start.2) | async-done | bytes 524320 | tf_op jit(solution)/shard_map/all_to_all | solution.py:139
  208.2 1.2 gather_fusion.2
  211.0 2.2 fusion.88
  213.2 1.7 convolution_convert_fusion.9
  214.9 1.7 convolution_convert_fusion.13
  216.6 2.2 multiply_reduce_fusion.3
  220.3 2.2 fusion.87
  222.5 1.7 convolution_convert_fusion.8
  224.2 1.7 convolution_convert_fusion.12
  225.9 2.2 multiply_reduce_fusion.2
  229.6 2.2 fusion.86
  231.8 1.7 convolution_convert_fusion.11
  233.5 2.2 multiply_reduce_fusion.1
  236.4 1.0 fusion.14
  237.4 0.9 fusion.10
  238.7 2.2 fusion.85
  240.9 1.7 convolution_convert_fusion.10
  242.6 2.2 multiply_reduce_fusion
  245.3 1.0 fusion.15
  246.3 0.9 fusion.11
  247.3 1.1 convolution_convert_fusion.2
  251.1 1.9 convolution_convert_fusion.7
  253.1 1.9 convolution_convert_fusion.6
  255.0 1.8 convolution_convert_fusion
  257.2 2.5 scatter_custom_fusion.1
  259.7 8.0 %all-to-all-start.1 = ((bf16[32,16,512]{2,1,0:T(8,128)(2,1)}), bf16[32,16,512]{2,1,0:T(8,128)(2,1)S(1)}, u32[]{:S(2)}, u32[]{:S(2)}) async-start(bf16[32,16,512]{2,1,0:T(8,128)(2,1)} %bitcast.28), calls=%async_computation.1 | async-start | bytes 1048576 | tf_op jit(solution)/shard_map/all_to_all | solution.py:131
  268.3 2.5 scatter_custom_fusion.3
  270.8 9.8 %all-to-all-done.1 = bf16[32,16,512]{2,1,0:T(8,128)(2,1)S(1)} async-done(((bf16[32,16,512]{2,1,0:T(8,128)(2,1)}), bf16[32,16,512]{2,1,0:T(8,128)(2,1)S(1)}, u32[]{:S(2)}, u32[]{:S(2)}) %all-to-all-start.1) | async-done | bytes 524320 | tf_op jit(solution)/shard_map/all_to_all | solution.py:131
  280.6 8.6 %all-to-all-start.3 = ((bf16[32,16,512]{2,1,0:T(8,128)(2,1)}), bf16[32,16,512]{2,1,0:T(8,128)(2,1)S(1)}, u32[]{:S(2)}, u32[]{:S(2)}) async-start(bf16[32,16,512]{2,1,0:T(8,128)(2,1)} %bitcast.62), calls=%async_computation.3 | async-start | bytes 1048576 | tf_op jit(solution)/shard_map/all_to_all | solution.py:156
  289.3 1.9 gather_fusion.1
  291.2 11.0 %all-to-all-done.3 = bf16[32,16,512]{2,1,0:T(8,128)(2,1)S(1)} async-done(((bf16[32,16,512]{2,1,0:T(8,128)(2,1)}), bf16[32,16,512]{2,1,0:T(8,128)(2,1)S(1)}, u32[]{:S(2)}, u32[]{:S(2)}) %all-to-all-start.3) | async-done | bytes 524320 | tf_op jit(solution)/shard_map/all_to_all | solution.py:156
  302.2 1.2 gather_fusion.3
  303.4 1.6 copy.151
  305.2 78.3 %all-reduce = (f32[512]{0:T(512)S(1)}, f32[512]{0:T(512)S(1)}) all-reduce(f32[512]{0:T(512)S(1)} %get-tuple-element.25, f32[512]{0:T(512)S(1)} %get-tuple-element.24), channel_id=1, replica_groups=mesh['region'=32,'group'=8] {'region','group'}, use_global_device_ids=true, to_apply=%region_23.24 | all-reduce | flops 1024 | bytes 8192 | tf_op jit(solution)/shard_map/psum | solution.py:164
  383.5 1.8 copy.149
  385.4 0.9 fusion.39
  386.3 121.8 %reduce-scatter.15.cloned.1.call-done = bf16[16,64]{1,0:T(8,128)(2,1)} async-done(((bf16[512,64]{1,0:T(8,128)(2,1)}), bf16[16,64]{1,0:T(8,128)(2,1)}) %reduce-scatter.15.cloned.1.call-update) | async-done | bytes 2064
  509.6 201.4 %reduce-scatter.13.cloned.1.call-done = bf16[48,64]{1,0:T(8,128)(2,1)} async-done(((bf16[1536,64]{1,0:T(8,128)(2,1)}), bf16[48,64]{1,0:T(8,128)(2,1)}) %reduce-scatter.13.cloned.1.call-update) | async-done | bytes 6160
  (135 shorter events, 14.1 us)
Async XLA Ops:
  7.2 202.7 %copy-start = (bf16[512,1536]{1,0:T(8,128)(2,1)S(1)}, bf16[512,1536]{1,0:T(8,128)(2,1)}, u32[]{:S(2)}) copy-start(bf16[512,1536]{1,0:T(8,128)(2,1)} %param.15) | copy-start | bytes 4718596
  7.2 165.6 %copy-start.11 = (bf16[1,256,512]{2,1,0:T(8,128)(2,1)S(1)}, bf16[1,256,512]{2,1,0:T(8,128)(2,1)}, u32[]{:S(2)}) copy-start(bf16[1,256,512]{2,1,0:T(8,128)(2,1)} %param.17) | copy-start | bytes 786436
  8.0 179.0 %copy-start.21 = (s32[256,1]{0,1:T(1,128)}, s32[256,1]{0,1:T(1,128)S(1)}, u32[]{:S(2)}) copy-start(s32[256,1]{0,1:T(1,128)S(1)} %compare_select_fusion) | copy-start | bytes 3076
  8.0 186.8 %copy-start.26 = (s32[1,256]{1,0:T(1,128)S(1)}, s32[1,256]{1,0:T(1,128)}, u32[]{:S(2)}) copy-start(s32[1,256]{1,0:T(1,128)} %param.11) | copy-start | bytes 3076
  8.0 186.8 %copy-start.20 = (s32[1,1,256]{2,1,0:T(1,128)S(1)}, s32[1,1,256]{2,1,0:T(1,128)}, u32[]{:S(2)}) copy-start(s32[1,1,256]{2,1,0:T(1,128)} %param.12) | copy-start | bytes 3076
  166.7 20.4 %all-to-all-start = ((bf16[32,16,512]{2,1,0:T(8,128)(2,1)}), bf16[32,16,512]{2,1,0:T(8,128)(2,1)S(1)}, u32[]{:S(2)}, u32[]{:S(2)}) async-start(bf16[32,16,512]{2,1,0:T(8,128)(2,1)} %bitcast.5), calls=%async_computation | async-start | bytes 1048576 | tf_op jit(solution)/shard_map/all_to_all | solution.py:119
  187.1 21.1 %all-to-all-start.2 = ((bf16[32,16,512]{2,1,0:T(8,128)(2,1)}), bf16[32,16,512]{2,1,0:T(8,128)(2,1)S(1)}, u32[]{:S(2)}, u32[]{:S(2)}) async-start(bf16[32,16,512]{2,1,0:T(8,128)(2,1)} %bitcast.32), calls=%async_computation.2 | async-start | bytes 1048576 | tf_op jit(solution)/shard_map/all_to_all | solution.py:139
  194.6 108.8 %reduce-scatter.11.cloned.1.call-start = ((), (), s32[]{:S(2)}) async-start(), calls=%async_computation.9 | async-start | bytes 589824 | tf_op jit(solution)/shard_map/reduce_scatter | solution.py:177
  194.8 14.5 %copy-start.23 = (s32[256,1]{0,1:T(1,128)}, s32[256,1]{0,1:T(1,128)S(1)}, u32[]{:S(2)}) copy-start(s32[256,1]{0,1:T(1,128)S(1)} %compare_select_fusion.1) | copy-start | bytes 3076
  195.0 29.2 %copy-start.12 = (pred[256,256]{0,1:T(8,128)(4,1)}, pred[256,256]{0,1:T(8,128)(4,1)S(1)}, u32[]{:S(2)}) copy-start(pred[256,256]{0,1:T(8,128)(4,1)S(1)} %broadcast_compare_fusion) | copy-start | bytes 196612
  195.0 14.4 %copy-start.6 = (bf16[512,512]{1,0:T(8,128)(2,1)S(1)}, bf16[512,512]{1,0:T(8,128)(2,1)}, u32[]{:S(2)}) copy-start(bf16[512,512]{1,0:T(8,128)(2,1)} %param.16) | copy-start | bytes 1572868
  216.6 2.2 copy-start.2
  225.9 2.2 copy-start.3
  228.5 1.1 copy-start.13
  229.3 4.3 copy-start.14
  233.5 2.2 copy-start.4
  238.4 4.3 copy-start.15
  240.9 3.9 copy-start.18
  242.6 2.3 copy-start.5
  245.3 1.9 copy-start.27
  245.3 1.9 copy-start.29
  245.3 1.9 copy-start.31
  245.3 1.9 copy-start.33
  245.3 3.1 copy-start.9
  246.3 3.0 copy-start.8
  247.2 2.2 copy-start.10
  248.4 135.1 %reduce-scatter.9.cloned.1.call-start = ((), (), s32[]{:S(2)}) async-start(), calls=%async_computation.8 | async-start | bytes 1769472 | tf_op jit(solution)/shard_map/reduce_scatter | solution.py:174
  251.1 2.0 copy-start.16
  251.1 2.0 copy-start.19
  255.0 1.9 copy-start.7
  255.0 1.9 copy-start.28
  255.0 1.9 copy-start.30
  255.0 1.9 copy-start.32
  255.0 1.9 copy-start.34
  259.7 21.0 %all-to-all-start.1 = ((bf16[32,16,512]{2,1,0:T(8,128)(2,1)}), bf16[32,16,512]{2,1,0:T(8,128)(2,1)S(1)}, u32[]{:S(2)}, u32[]{:S(2)}) async-start(bf16[32,16,512]{2,1,0:T(8,128)(2,1)} %bitcast.28), calls=%async_computation.1 | async-start | bytes 1048576 | tf_op jit(solution)/shard_map/all_to_all | solution.py:131
  267.7 21.6 %copy-start.22 = (s32[256,1]{0,1:T(1,128)S(1)}, s32[256,1]{0,1:T(1,128)}, u32[]{:S(2)}) copy-start(s32[256,1]{0,1:T(1,128)} %copy-done.21) | copy-start | bytes 3076
  280.6 21.6 %all-to-all-start.3 = ((bf16[32,16,512]{2,1,0:T(8,128)(2,1)}), bf16[32,16,512]{2,1,0:T(8,128)(2,1)S(1)}, u32[]{:S(2)}, u32[]{:S(2)}) async-start(bf16[32,16,512]{2,1,0:T(8,128)(2,1)} %bitcast.62), calls=%async_computation.3 | async-start | bytes 1048576 | tf_op jit(solution)/shard_map/all_to_all | solution.py:156
  289.2 218.9 %reduce-scatter.15.cloned.1.call-start = ((), (), s32[]{:S(2)}) async-start(), calls=%async_computation.11 | async-start | bytes 135168
  289.3 15.8 %copy-start.1 = (bf16[1,256,512]{2,1,0:T(8,128)(2,1)S(1)}, bf16[1,256,512]{2,1,0:T(8,128)(2,1)}, u32[]{:S(2)}) copy-start(bf16[1,256,512]{2,1,0:T(8,128)(2,1)} %param.9) | copy-start | bytes 786436
  302.2 83.2 %copy-start.17 = (f32[512]{0:T(512)S(1)}, f32[512]{0:T(512)}, u32[]{:S(2)}) copy-start(f32[512]{0:T(512)} %param.13) | copy-start | bytes 6148
  305.0 405.9 %reduce-scatter.13.cloned.1.call-start = ((), (), s32[]{:S(2)}) async-start(), calls=%async_computation.10 | async-start | bytes 405504
  383.5 328.9 %copy-start.24 = (f32[512]{0:T(512)}, f32[512]{0:T(512)S(1)}, u32[]{:S(2)}) copy-start(f32[512]{0:T(512)S(1)} %get-tuple-element.26) | copy-start | bytes 6148
  383.5 328.9 %copy-start.25 = (f32[512]{0:T(512)}, f32[512]{0:T(512)S(1)}, u32[]{:S(2)}) copy-start(f32[512]{0:T(512)S(1)} %get-tuple-element.27) | copy-start | bytes 6148
Sparse Core Ops, SparseCore 0:
  248.5 29.7 reduce-scatter.10
  281.0 34.5 reduce-scatter.8
  319.7 188.3 reduce-scatter.14
  511.8 199.1 reduce-scatter.12
where the time goes:
time: 725 us; the launch traced here: 719 us
  waiting for transfers between devices  368 us (51%)
  blocking collectives  232 us (32%)
  matrix products  41.4 us (6%)
  starting transfers between devices  30.5 us (4%)
  local copies, waits for them, and re-layouts  23.7 us (3%)
  between operations  14.5 us (2%)
  other arithmetic  8.56 us (1%)
    unnamed x6, waiting for transfers between devices  323 us
    psum x1, blocking collectives, on_device(): lax.psum(jnp.sum(local_rows, axis=0), ('region', 'group')) / count_all  81.4 us
    psum x1, blocking collectives, on_device(): lax.psum((jnp.sum(grad_normed, axis=0), jnp.sum(grad_normed * unit_rows,...  78.3 us
    psum x1, blocking collectives, on_device(): lax.psum(jnp.sum(centered * centered, axis=0), ('region', 'group'))  72.4 us
  transfers between devices with their start and end apart: 8, of which 6 were waited for; matrix products, arithmetic and copies ran while one was open for 4% of the time, Pallas kernels for 0%

commit v1 on v0

v1 whole, which is shorter than its diff:
```python
import functools

import jax
import jax.numpy as jnp
from jax import lax
from jax.experimental import pallas as pl
from jax.experimental.pallas import tpu as pltpu
from jax.sharding import PartitionSpec as P

HEAD_DIM = 16
EPS = 1e-05
PTS = 256
WIDTH = 512
CAP = 16
REGIONS = 32
GROUPS = 8
TOTAL = 65536
MESH = pl.DeviceIdType.MESH
BF = jnp.bfloat16
F32 = jnp.float32


def dot_nn(a, b):
    return jnp.dot(a, b, preferred_element_type=F32)


def dot_nt(a, b):
    return lax.dot_general(a, b, (((1,), (1,)), ((), ())), preferred_element_type=F32)


def as_column(row):
    return jnp.broadcast_to(row, (128, row.shape[1])).T


def slot_rows(row):
    slots = lax.broadcasted_iota(jnp.int32, (REGIONS * CAP, PTS), 0)
    return jnp.where(slots == row, 1.0, 0.0).astype(BF)


def slot_columns(row):
    col = as_column(row.astype(F32)).astype(jnp.int32)
    lane = lax.broadcasted_iota(jnp.int32, (PTS, 128), 1)
    parts = [jnp.where(col == lane + 128 * j, 1.0, 0.0) for j in range(4)]
    return jnp.concatenate(parts, axis=1).astype(BF)


def store_rows(ref, at, first, row):
    for j in range(4):
        ref[at, first + j : first + j + 1, :] = row[:, 128 * j : 128 * (j + 1)]


def load_row(block, first):
    return jnp.concatenate([block[first + j : first + j + 1, :] for j in range(4)], axis=1)


def kernel(
    x_ref, rs_ref, ps_ref, pid_ref, gain_ref, bias_ref, wqkv_hbm, wproj_hbm, cot_ref,
    out_ref, gp_ref, gwq_ref, gwp_ref, gg_ref, gb_ref,
    wqkv, wproj, w_sem,
    send_a, recv_a, send_b, recv_b, send_c, recv_c, send_d, recv_d,
    st1, st2, gs1, gs2,
    p_t, q_n, q_t, patch_bias,
    unit_s, serial, qkv, qs, kt, vt, probs, mixed_t, mixed,
    g_serial_t, gm, big_w, big_d, stack_g, stack_q, gqkv, gqkv_t,
    g32, g_core, r_core, s_x, r_x, s_r, r_r, fin, fin_t,
    send_sems, recv_sems,
):
    r = lax.axis_index("region")
    g = lax.axis_index("group")
    xx = g // 2
    core = g % 2

    def each_region(act):
        def body(k, carry):
            act(lax.rem(r + k, REGIONS))
            return carry

        lax.fori_loop(1, REGIONS, body, 0)

    def each_group(act):
        def body(k, carry):
            act(lax.rem(g + k, GROUPS))
            return carry

        lax.fori_loop(1, GROUPS, body, 0)

    def send(src, dst, stage, to):
        pltpu.make_async_remote_copy(
            src_ref=src, dst_ref=dst, send_sem=send_sems.at[stage], recv_sem=recv_sems.at[stage],
            device_id=to, device_id_type=MESH,
        ).start()

    def wait(ref, sem):
        pltpu.make_async_copy(ref, ref, sem).wait()

    barrier = pltpu.get_barrier_semaphore()
    each_region(
        lambda p: pl.semaphore_signal(barrier, inc=1, device_id=(p, g), device_id_type=MESH)
    )
    each_group(
        lambda p: pl.semaphore_signal(barrier, inc=1, device_id=(r, p), device_id_type=MESH)
    )
    load_qkv = pltpu.make_async_copy(wqkv_hbm, wqkv, w_sem.at[0])
    load_proj = pltpu.make_async_copy(wproj_hbm, wproj, w_sem.at[1])
    load_qkv.start()
    load_proj.start()

    x = x_ref[...]
    xf = x.astype(F32)
    mean_l = jnp.sum(xf, axis=0, keepdims=True) * (1.0 / PTS)
    dev = xf - mean_l
    store_rows(st1, g, 0, mean_l)
    store_rows(st1, g, 4, jnp.sum(dev * dev, axis=0, keepdims=True))
    p_n = slot_rows(rs_ref[...])
    send_a[...] = dot_nn(p_n, x).astype(BF).reshape(REGIONS, CAP, WIDTH)

    pl.semaphore_wait(barrier, REGIONS - 1 + GROUPS - 1)

    each_group(lambda p: send(st1.at[g], st1.at[g], 0, (r, p)))
    each_region(lambda p: send(send_a.at[p], recv_a.at[r], 1, (p, g)))
    recv_a[r] = send_a[r]

    send_b[...] = dot_nn(p_n, cot_ref[...]).astype(BF).reshape(REGIONS, CAP, WIDTH)
    p_t[...] = slot_columns(rs_ref[...])
    q_n[...] = slot_rows(ps_ref[...])
    q_t[...] = slot_columns(ps_ref[...])
    pid_row = pid_ref[...]
    pid_col = as_column(pid_row.astype(F32)).astype(jnp.int32)
    patch_bias[...] = jnp.concatenate(
        [
            jnp.where(pid_col == pid_row[:, 128 * j : 128 * (j + 1)], 0.0, -1e30)
            for j in range(2)
        ],
        axis=1,
    )

    wait(st1.at[pl.ds(0, GROUPS - 1)], recv_sems.at[0])

    def merge(block, count, each):
        means, squares = block[:, 0:4, :], block[:, 4:8, :]
        mean = jnp.sum(means, axis=0) * (1.0 / count)
        off = means - mean[None]
        return mean, jnp.sum(squares, axis=0) + each * jnp.sum(off * off, axis=0)

    mean_g, square_g = merge(st1[...], GROUPS, float(PTS))
    st2[r, 0:4, :] = mean_g
    st2[r, 4:8, :] = square_g
    each_region(lambda p: send(st2.at[r], st2.at[r], 2, (p, g)))

    each_region(lambda p: send(send_b.at[p], recv_b.at[r], 3, (p, g)))
    recv_b[r] = send_b[r]

    wait(st2.at[pl.ds(0, REGIONS - 1)], recv_sems.at[2])
    mean_4, square_4 = merge(st2[...], REGIONS, float(PTS * GROUPS))
    inv_4 = lax.rsqrt(square_4 * (1.0 / TOTAL) + EPS)
    mean_all = load_row(mean_4, 0)
    inv_std = load_row(inv_4, 0)
    gain = gain_ref[...]

    wait(recv_a.at[pl.ds(0, REGIONS - 1)], recv_sems.at[1])
    pts = dot_nn(q_t[...], recv_a[...].reshape(REGIONS * CAP, WIDTH))
    unit = (pts - mean_all) * inv_std
    unit_s[...] = unit
    serial[...] = (unit * gain + bias_ref[...]).astype(BF)

    load_qkv.wait()
    load_proj.wait()
    qkv[...] = dot_nn(serial[...], wqkv[...]).astype(BF)
    qs[...] = qkv[:, 0:WIDTH] * jnp.asarray(0.25, BF)
    kt[...] = qkv[:, WIDTH : 2 * WIDTH].T
    vt[...] = qkv[:, 2 * WIDTH : 3 * WIDTH].T

    lane_head = lax.broadcasted_iota(jnp.int32, (1, 128), 1) // HEAD_DIM

    def head_mask(h):
        return jnp.where(lane_head == h, 1.0, 0.0).astype(BF)

    def forward(chunk, carry):
        col = pl.multiple_of(chunk * 128, 128)
        keys = qkv[:, pl.ds(WIDTH + col, 128)]
        queries = qs[:, pl.ds(col, 128)]
        for h in range(8):
            scores = dot_nt(keys * head_mask(h), queries) + patch_bias[...]
            raised = jnp.exp(scores - jnp.max(scores, axis=0, keepdims=True))
            p = raised * (1.0 / jnp.sum(raised, axis=0, keepdims=True))
            probs[chunk * 8 + h] = p
            rows = pl.ds(pl.multiple_of(col + HEAD_DIM * h, HEAD_DIM), HEAD_DIM)
            mixed_t[rows, :] = dot_nn(vt[rows, :], p.astype(BF)).astype(BF)
        return carry

    lax.fori_loop(0, 4, forward, 0)
    mixed[...] = mixed_t[...].T
    branch = dot_nn(mixed[...], wproj[...]).astype(BF)
    send_c[...] = dot_nn(q_n[...], branch).astype(BF).reshape(REGIONS, CAP, WIDTH)
    each_region(lambda p: send(send_c.at[p], recv_c.at[r], 4, (p, g)))
    recv_c[r] = send_c[r]

    wait(recv_b.at[pl.ds(0, REGIONS - 1)], recv_sems.at[3])
    g_serial = dot_nn(q_t[...], recv_b[...].reshape(REGIONS * CAP, WIDTH)).astype(BF)
    g_serial_t[...] = g_serial.T
    gm[...] = dot_nt(g_serial, wproj[...]).astype(BF)

    def backward(chunk, carry):
        col = pl.multiple_of(chunk * 128, 128)
        values = qkv[:, pl.ds(2 * WIDTH + col, 128)]
        grads = gm[:, pl.ds(col, 128)]
        queries = qs[:, pl.ds(col, 128)]
        for h in range(8):
            mask = head_mask(h)
            span = slice(PTS * h, PTS * (h + 1))
            grad_w = dot_nt(values * mask, grads)
            p = probs[chunk * 8 + h]
            total = jnp.sum(p * grad_w, axis=0, keepdims=True)
            ds = (p * (grad_w - total)).astype(BF)
            big_w[:, span] = p.astype(BF)
            big_d[:, span] = ds
            stack_g[span, :] = grads * mask
            stack_q[span, :] = queries * mask
            rows = pl.ds(pl.multiple_of(col + HEAD_DIM * h, HEAD_DIM), HEAD_DIM)
            gqkv_t[rows, :] = (dot_nn(kt[rows, :], ds) * 0.25).astype(BF)
        gqkv[:, pl.ds(WIDTH + col, 128)] = dot_nn(big_d[...], stack_q[...]).astype(BF)
        gqkv[:, pl.ds(2 * WIDTH + col, 128)] = dot_nn(big_w[...], stack_g[...]).astype(BF)
        return carry

    lax.fori_loop(0, 4, backward, 0)
    gqkv[:, 0:WIDTH] = gqkv_t[0:WIDTH, :].T
    gqkv_t[WIDTH : 3 * WIDTH, :] = gqkv[:, WIDTH : 3 * WIDTH].T

    def weight_grads(part, carry):
        q_rows = dot_nn(gqkv_t[pl.ds(pl.multiple_of(part * 384, 384), 384), :], serial[...])
        p_rows = dot_nn(g_serial_t[pl.ds(pl.multiple_of(part * 128, 128), 128), :], mixed[...])
        for i in range(8):
            low = pl.multiple_of(part * 256 + i * 32, 32)
            for b in range(4):
                cols = slice(128 * b, 128 * (b + 1))
                g32[0, b, pl.ds(low, 32), :] = q_rows[48 * i : 48 * i + 32, cols]
                g32[1, b, pl.ds(low, 16), :] = q_rows[48 * i + 32 : 48 * i + 48, cols]
                g32[1, b, pl.ds(low + 16, 16), :] = p_rows[16 * i : 16 * i + 16, cols]
        return carry

    lax.fori_loop(0, 4, weight_grads, 0)
    g_core[...] = g32[1 - core].astype(BF)
    sibling = (r, xx * 2 + 1 - core)
    send(g_core, r_core, 5, sibling)

    grad_in = dot_nt(gqkv[...], wqkv[...]).astype(BF)
    send_d[...] = dot_nn(q_n[...], grad_in).astype(BF).reshape(REGIONS, CAP, WIDTH)
    grad_f = grad_in.astype(F32)
    store_rows(gs1, g, 0, jnp.sum(grad_f, axis=0, keepdims=True))
    store_rows(gs1, g, 4, jnp.sum(grad_f * unit_s[...], axis=0, keepdims=True))
    each_group(lambda p: send(gs1.at[g], gs1.at[g], 6, (r, p)))
    each_region(lambda p: send(send_d.at[p], recv_d.at[r], 7, (p, g)))
    recv_d[r] = send_d[r]

    wait(r_core, recv_sems.at[5])
    for b in range(4):
        s_x[b] = (g32[core, b] + r_core[b].astype(F32)).astype(BF)
    for k in range(1, 4):
        xp = lax.rem(xx + k, 4)
        send(s_x.at[xp], r_x.at[xx], 8, (r, xp * 2 + core))

    wait(gs1.at[pl.ds(0, GROUPS - 1)], recv_sems.at[6])
    gs2[r] = jnp.sum(gs1[...], axis=0)
    each_region(lambda p: send(gs2.at[r], gs2.at[r], 9, (p, g)))

    wait(recv_c.at[pl.ds(0, REGIONS - 1)], recv_sems.at[4])
    out_ref[...] = dot_nn(p_t[...], recv_c[...].reshape(REGIONS * CAP, WIDTH)).astype(BF)

    wait(r_x.at[pl.ds(0, 3)], recv_sems.at[8])
    mine = g32[core, xx] + r_core[xx].astype(F32)
    for k in range(1, 4):
        mine = mine + r_x[lax.rem(xx + k, 4)].astype(F32)
    s_r[...] = mine.astype(BF).reshape(REGIONS, 32, 128)
    each_region(lambda p: send(s_r.at[p], r_r.at[r], 10, (p, g)))
    r_r[r] = s_r[r]

    wait(gs2.at[pl.ds(0, REGIONS - 1)], recv_sems.at[9])
    sums = jnp.sum(gs2[...], axis=0)
    grad_bias = load_row(sums, 0)
    grad_gain = load_row(sums, 4)
    gb_ref[...] = grad_bias
    gg_ref[...] = grad_gain

    wait(recv_d.at[pl.ds(0, REGIONS - 1)], recv_sems.at[7])
    grad_n = dot_nn(p_t[...], recv_d[...].reshape(REGIONS * CAP, WIDTH))
    unit_b = (x_ref[...].astype(F32) - mean_all) * inv_std
    scale = 1.0 / TOTAL
    gp_ref[...] = (
        inv_std
        * (grad_n * gain - gain * grad_bias * scale - unit_b * (gain * grad_gain * scale))
    ).astype(BF)

    wait(r_r.at[pl.ds(0, REGIONS - 1)], recv_sems.at[10])
    fin[2:4] = jnp.zeros((2, 32, 128), F32)
    fin[core] = jnp.sum(r_r[...].astype(F32), axis=0)
    send(fin.at[core], fin.at[core], 11, sibling)
    wait(fin.at[0], recv_sems.at[11])
    fin_t[...] = fin[...].reshape(128, 128).T
    own = fin_t[pl.ds(pl.multiple_of(core * 64, 64), 64), :]
    gwq_ref[...] = own[:, 0:48]
    gwp_ref[...] = own[:, 48:64]

    wait(st1.at[pl.ds(0, GROUPS - 1)], send_sems.at[0])
    wait(send_a.at[pl.ds(0, REGIONS - 1)], send_sems.at[1])
    wait(st2.at[pl.ds(0, REGIONS - 1)], send_sems.at[2])
    wait(send_b.at[pl.ds(0, REGIONS - 1)], send_sems.at[3])
    wait(send_c.at[pl.ds(0, REGIONS - 1)], send_sems.at[4])
    wait(g_core, send_sems.at[5])
    wait(gs1.at[pl.ds(0, GROUPS - 1)], send_sems.at[6])
    wait(send_d.at[pl.ds(0, REGIONS - 1)], send_sems.at[7])
    wait(s_x.at[pl.ds(0, 3)], send_sems.at[8])
    wait(gs2.at[pl.ds(0, REGIONS - 1)], send_sems.at[9])
    wait(s_r.at[pl.ds(0, REGIONS - 1)], send_sems.at[10])
    wait(fin.at[0], send_sems.at[11])


def on_device(points, row_slot, pos_slot, patch_ids, bn_gain, bn_bias, w_qkv, w_proj, cotangent):
    vmem = pl.BlockSpec(memory_space=pltpu.VMEM)
    hbm = pl.BlockSpec(memory_space=pl.ANY)
    slots = (REGIONS, CAP, WIDTH)
    scratch = [
        pltpu.VMEM((WIDTH, 3 * WIDTH), BF),
        pltpu.VMEM((WIDTH, WIDTH), BF),
        pltpu.SemaphoreType.DMA((2,)),
        *[pltpu.VMEM(slots, BF) for _ in range(8)],
        pltpu.VMEM((GROUPS, 8, 128), F32),
        pltpu.VMEM((REGIONS, 8, 128), F32),
        pltpu.VMEM((GROUPS, 8, 128), F32),
        pltpu.VMEM((REGIONS, 8, 128), F32),
        pltpu.VMEM((PTS, WIDTH), BF),
        pltpu.VMEM((WIDTH, PTS), BF),
        pltpu.VMEM((PTS, WIDTH), BF),
        pltpu.VMEM((PTS, PTS), F32),
        pltpu.VMEM((PTS, WIDTH), F32),
        pltpu.VMEM((PTS, WIDTH), BF),
        pltpu.VMEM((PTS, 3 * WIDTH), BF),
        pltpu.VMEM((PTS, WIDTH), BF),
        pltpu.VMEM((WIDTH, PTS), BF),
        pltpu.VMEM((WIDTH, PTS), BF),
        pltpu.VMEM((32, PTS, PTS), F32),
        pltpu.VMEM((WIDTH, PTS), BF),
        pltpu.VMEM((PTS, WIDTH), BF),
        pltpu.VMEM((WIDTH, PTS), BF),
        pltpu.VMEM((PTS, WIDTH), BF),
        pltpu.VMEM((PTS, 8 * PTS), BF),
        pltpu.VMEM((PTS, 8 * PTS), BF),
        pltpu.VMEM((8 * PTS, 128), BF),
        pltpu.VMEM((8 * PTS, 128), BF),
        pltpu.VMEM((PTS, 3 * WIDTH), BF),
        pltpu.VMEM((3 * WIDTH, PTS), BF),
        pltpu.VMEM((2, 4, 1024, 128), F32),
        pltpu.VMEM((4, 1024, 128), BF),
        pltpu.VMEM((4, 1024, 128), BF),
        pltpu.VMEM((4, 1024, 128), BF),
        pltpu.VMEM((4, 1024, 128), BF),
        pltpu.VMEM((REGIONS, 32, 128), BF),
        pltpu.VMEM((REGIONS, 32, 128), BF),
        pltpu.VMEM((4, 32, 128), F32),
        pltpu.VMEM((128, 128), F32),
        pltpu.SemaphoreType.DMA((12,)),
        pltpu.SemaphoreType.DMA((12,)),
    ]
    output, grad_points, grad_qkv, grad_proj, grad_gain, grad_bias = pl.pallas_call(
        kernel,
        out_shape=[
            jax.ShapeDtypeStruct((PTS, WIDTH), BF),
            jax.ShapeDtypeStruct((PTS, WIDTH), BF),
            jax.ShapeDtypeStruct((64, 48), F32),
            jax.ShapeDtypeStruct((64, 16), F32),
            jax.ShapeDtypeStruct((1, WIDTH), F32),
            jax.ShapeDtypeStruct((1, WIDTH), F32),
        ],
        in_specs=[vmem] * 6 + [hbm, hbm, vmem],
        out_specs=[vmem] * 6,
        scratch_shapes=scratch,
        compiler_params=pltpu.CompilerParams(
            collective_id=0, has_side_effects=True, vmem_limit_bytes=52 * 1024 * 1024
        ),
    )(
        points[0], row_slot, pos_slot, patch_ids[0], bn_gain[None], bn_bias[None],
        w_qkv, w_proj, cotangent[0],
    )
    return output[None], grad_points[None], grad_qkv, grad_proj, grad_gain[0], grad_bias[0]


def solution(mesh):
    placed = (
        P("group", "region", None),
        P("group", "region"),
        P("group", "region"),
        P("group", "region", None),
        P(),
        P(),
        P(),
        P(),
        P("group", "region", None),
    )
    return jax.shard_map(
        on_device,
        mesh=mesh,
        in_specs=placed,
        out_specs=(
            P("group", "region", None),
            P("group", "region", None),
            P("group", "region"),
            P("group", "region"),
            P(),
            P(),
        ),
        check_vma=False,
    )
```

time: 725 us -> 95.7 us (0.13)
  waiting for transfers between devices: 368 us -> 0 us
  blocking collectives: 232 us -> 0 us
  Pallas kernels: 0 us -> 84.5 us
  matrix products: 41.4 us -> 0 us
  starting transfers between devices: 30.5 us -> 0 us
  between operations: 14.5 us -> 0.66 us
  local copies, waits for them, and re-layouts: 23.7 us -> 10.2 us
  other arithmetic: 8.56 us -> 0 us
    unnamed x6 -> x0, waiting for transfers between devices: 323 us -> none
    psum x3 -> x0, blocking collectives: 232 us -> none  [the longest x1 81.4 us: on_device(): lax.psum(jnp.sum(local_rows, axis=0), ('region', 'group')) / count_all]
    pallas_call x0 -> x1, Pallas kernels: none -> 84.5 us  [on_device(): pl.pallas_call(kernel, out_shape=[jax.ShapeDtypeStruct((PTS, WIDTH), BF),...]
    all_to_all x4 -> x0, waiting for transfers between devices: 44.9 us -> none  [the longest x1 12 us: on_device(): lax.all_to_all(to_slots(grad_home_rows, send_rows, region_size, capacity)...]
    dot_general x26 -> x0, matrix products: 32.6 us -> none  [the longest x4 8.91 us: attend_backward(): jnp.einsum('qhd,khd->hqk', grad_heads, value_heads, preferred_element_typ...]
    all_to_all x4 -> x0, starting transfers between devices: 30.2 us -> none  [the longest x1 8.57 us: on_device(): lax.all_to_all(to_slots(grad_serial_in, recv_rows, region_size, capacity)...]
    sub x4 -> x0, matrix products: 8.8 us -> none  [masked_softmax(): raised = jnp.exp(scores - highest)]
    scatter x3 -> x0, local copies, waits for them, and re-layouts: 7.26 us -> none  [to_slots(): filled = jnp.zeros((region_size * capacity, rows_in.shape[1]), rows_in.dt...]
  transfers between devices with their start and end apart: 8 -> 0, of which waited for: 6 -> 0; matrix products, arithmetic and copies ran while one was open for 4% -> 0% of each run, Pallas kernels for 0% -> 0%
where the time goes in v1:
time: 95.7 us; the launch traced here: 95.4 us
  Pallas kernels  84.5 us (88%)
  local copies, waits for them, and re-layouts  10.2 us (11%)
    pallas_call x1, Pallas kernels, on_device(): pl.pallas_call(kernel, out_shape=[jax.ShapeDtypeStruct((PTS, WIDTH), BF),...  84.5 us
    unnamed x22, local copies, waits for them, and re-layouts  10.2 us

profile of v1, /device:TPU:1, one launch (start us, length us, event | category | flops | bytes accessed | tf_op | source)
XLA Modules:
  0.0 95.4 jit_solution(9191138018814622995)
XLA Ops:
  0.6 0.0 copy-start
  0.6 1.0 %copy-done = bf16[512,512]{1,0:T(8,128)(2,1)S(1)} copy-done((bf16[512,512]{1,0:T(8,128)(2,1)S(1)}, bf16[512,512]{1,0:T(8,128)(2,1)}, u32[]{:S(2)}) %copy-start) | copy-done | bytes 524312
  1.7 0.0 copy-start.1
  1.7 0.9 copy-done.1
  2.6 0.0 copy-start.2
  2.6 0.9 copy-done.2
  3.6 0.0 copy-start.3
  3.6 0.7 copy-done.3
  4.3 0.0 copy-start.4
  4.3 0.7 copy-done.4
  4.9 0.0 copy-start.5
  4.9 0.7 copy-done.5
  5.6 0.0 copy-start.6
  5.6 0.7 copy-done.6
  6.3 0.0 copy-start.7
  6.3 0.7 copy-done.7
  7.0 84.5 %shard_map.136 = (bf16[256,512]{1,0:T(8,128)(2,1)S(1)}, bf16[256,512]{1,0:T(8,128)(2,1)S(1)}, f32[64,48]{1,0:T(8,128)S(1)}, f32[64,16]{1,0:T(8,128)S(1)}, f32[1,512]{1,0:T(1,128)S(1)}, /*index=5*/f32[1,512]{1,0:T(1,128)S(1)}) custom-call(bf16[256,512]{1,0:T(8,128)(2,1)S(1)} %bitcast.11, s32[1,256]{1,0:T(1,128)S(1)} %copy-done.5, s32[1,256]{1,0:T(1,128)S(1)} %copy-done.6, ...), custom_call_target="tpu_custom_call" | custom-call | tf_op jit(solution)/shard_map/pallas_call | solution.py:363
  91.5 0.7 copy.16
  92.2 0.7 copy.15
  92.9 0.7 copy.21
  93.6 0.7 copy.22
  94.3 0.6 copy.23
  94.8 0.6 copy.24
Async XLA Ops:
  0.6 1.0 %copy-start = (bf16[512,512]{1,0:T(8,128)(2,1)S(1)}, bf16[512,512]{1,0:T(8,128)(2,1)}, u32[]{:S(2)}) copy-start(bf16[512,512]{1,0:T(8,128)(2,1)} %wproj_hbm.1) | copy-start | bytes 1572868
  1.7 0.9 copy-start.1
  2.6 0.9 copy-start.2
  3.6 0.7 copy-start.3
  4.3 0.7 copy-start.4
  4.9 0.7 copy-start.5
  5.6 0.7 copy-start.6
  6.3 0.7 copy-start.7

commit v2 on v1

v2 whole, which is shorter than its diff:
```python
import functools

import jax
import jax.numpy as jnp
from jax import lax
from jax.experimental import pallas as pl
from jax.experimental.pallas import tpu as pltpu
from jax.sharding import PartitionSpec as P

HEAD_DIM = 16
EPS = 1e-05
PTS = 256
WIDTH = 512
CAP = 16
REGIONS = 32
GROUPS = 8
YS, ZS = 4, 8
CHUNK = 192
TOTAL = 65536
MESH = pl.DeviceIdType.MESH
BF = jnp.bfloat16
F32 = jnp.float32


def dot_nn(a, b):
    return jnp.dot(a, b, preferred_element_type=F32)


def dot_nt(a, b):
    return lax.dot_general(a, b, (((1,), (1,)), ((), ())), preferred_element_type=F32)


def as_column(row):
    return jnp.broadcast_to(row.astype(F32), (128, row.shape[1])).T.astype(jnp.int32)


def slot_rows(row):
    slots = lax.broadcasted_iota(jnp.int32, (REGIONS * CAP, PTS), 0)
    return jnp.where(slots == row, 1.0, 0.0).astype(BF)


def slot_columns(row):
    col = as_column(row)
    lane = lax.broadcasted_iota(jnp.int32, (PTS, 128), 1)
    parts = [jnp.where(col == lane + 128 * j, 1.0, 0.0) for j in range(4)]
    return jnp.concatenate(parts, axis=1).astype(BF)


def store_rows(ref, at, first, row):
    for j in range(4):
        ref[at, first + j : first + j + 1, :] = row[:, 128 * j : 128 * (j + 1)]


def load_row(block, first):
    return jnp.concatenate([block[first + j : first + j + 1, :] for j in range(4)], axis=1)


def kernel(
    x_hbm, rs_hbm, ps_hbm, pid_hbm, gain_hbm, bias_hbm, wqkv_hbm, wproj_hbm, cot_hbm,
    out_ref, gp_ref, gwq_ref, gwp_ref, gg_ref, gb_ref,
    x_ref, rs_ref, ps_ref, pid_ref, gain_ref, bias_ref, wqkv, wproj, cot_ref, in_sems,
    send_a, recv_a, send_b, recv_b, send_c, recv_c, send_d, recv_d,
    st1, st2, st3, gs1, gs2, gs3,
    p_t, q_n, q_t, aug_k, query_x, grad_x,
    unit_s, serial, qkv, qs, kt, value_x, es, heads, mixed_f, mixed_t, mixed,
    g_serial_t, gm, big_d, stack_g, stack_q, gqkv, left,
    g32, g_core, r_core, s_x, r_x, acc, s_y, r_y, s_z, r_z, fin,
    send_sems, recv_sems, core_send, core_recv, x_send, x_recv,
):
    r = lax.axis_index("region")
    g = lax.axis_index("group")
    xx, core = g // 2, g % 2
    yy, zz = r // ZS, r % ZS

    def each_region(act):
        def body(k, carry):
            act(lax.rem(r + k, REGIONS))
            return carry

        lax.fori_loop(1, REGIONS, body, 0)

    def each_group(act):
        def body(k, carry):
            act(lax.rem(g + k, GROUPS))
            return carry

        lax.fori_loop(1, GROUPS, body, 0)

    def remote(src, dst, send_sem, recv_sem, to):
        pltpu.make_async_remote_copy(
            src_ref=src, dst_ref=dst, send_sem=send_sem, recv_sem=recv_sem,
            device_id=to, device_id_type=MESH,
        ).start()

    def send(src, dst, stage, to):
        remote(src, dst, send_sems.at[stage], recv_sems.at[stage], to)

    def wait(ref, sem):
        pltpu.make_async_copy(ref, ref, sem).wait()

    def along_y(buf, stage):
        for k in range(1, YS):
            yp = lax.rem(yy + k, YS)
            send(buf.at[yy], buf.at[yy], stage, (yp * ZS + zz, g))

    def along_z(buf, stage):
        for k in range(1, ZS):
            zp = lax.rem(zz + k, ZS)
            send(buf.at[zz], buf.at[zz], stage, (yy * ZS + zp, g))

    def others(buf):
        return buf.at[pl.ds(0, buf.shape[0] - 1)]

    barrier = pltpu.get_barrier_semaphore()
    each_region(
        lambda p: pl.semaphore_signal(barrier, inc=1, device_id=(p, g), device_id_type=MESH)
    )
    each_group(
        lambda p: pl.semaphore_signal(barrier, inc=1, device_id=(r, p), device_id_type=MESH)
    )
    loads = [
        pltpu.make_async_copy(src, dst, in_sems.at[i])
        for i, (src, dst) in enumerate(
            [
                (rs_hbm, rs_ref), (x_hbm, x_ref), (ps_hbm, ps_ref), (pid_hbm, pid_ref),
                (cot_hbm, cot_ref), (gain_hbm, gain_ref), (bias_hbm, bias_ref),
                (wqkv_hbm, wqkv), (wproj_hbm, wproj),
            ]
        )
    ]
    for load in loads:
        load.start()

    loads[0].wait()
    p_n = slot_rows(rs_ref[...])
    loads[1].wait()
    x = x_ref[...]
    send_a[...] = dot_nn(p_n, x).astype(BF).reshape(REGIONS, CAP, WIDTH)

    pl.semaphore_wait(barrier, REGIONS - 1 + GROUPS - 1)

    each_region(lambda p: send(send_a.at[p], recv_a.at[r], 1, (p, g)))
    recv_a[r] = send_a[r]

    xf = x.astype(F32)
    mean_l = jnp.sum(xf, axis=0, keepdims=True) * (1.0 / PTS)
    dev = xf - mean_l
    store_rows(st1, g, 0, mean_l)
    store_rows(st1, g, 4, jnp.sum(dev * dev, axis=0, keepdims=True))
    each_group(lambda p: send(st1.at[g], st1.at[g], 0, (r, p)))

    for load in loads[2:]:
        load.wait()
    p_t[...] = slot_columns(rs_ref[...])
    q_n[...] = slot_rows(ps_ref[...])
    q_t[...] = slot_columns(ps_ref[...])
    send_b[...] = dot_nn(p_n, cot_ref[...]).astype(BF).reshape(REGIONS, CAP, WIDTH)
    pid_row = pid_ref[...]
    lane = lax.broadcasted_iota(jnp.int32, (PTS, 128), 1)
    aug_k[...] = jnp.where(
        (lane < 4) & (as_column(pid_row) != lane), -1e30, 0.0
    ).astype(BF)
    row = lax.broadcasted_iota(jnp.int32, (128, PTS), 0)
    same = jnp.where(row == pid_row, 1.0, 0.0).astype(BF)
    for j in range(4):
        query_x[j, 128:256, :] = same

    def merge(block, count, each):
        means, squares = block[:, 0:4, :], block[:, 4:8, :]
        mean = jnp.sum(means, axis=0) * (1.0 / count)
        off = means - mean[None]
        return mean, jnp.sum(squares, axis=0) + each * jnp.sum(off * off, axis=0)

    wait(others(st1), recv_sems.at[0])
    st2[yy, 0:4, :], st2[yy, 4:8, :] = merge(st1[...], GROUPS, float(PTS))
    along_y(st2, 2)
    wait(others(st2), recv_sems.at[2])
    st3[zz, 0:4, :], st3[zz, 4:8, :] = merge(st2[...], YS, float(PTS * GROUPS))
    along_z(st3, 9)

    each_region(lambda p: send(send_b.at[p], recv_b.at[r], 3, (p, g)))
    recv_b[r] = send_b[r]

    wait(others(st3), recv_sems.at[9])
    mean_4, square_4 = merge(st3[...], ZS, float(PTS * GROUPS * YS))
    inv_4 = lax.rsqrt(square_4 * (1.0 / TOTAL) + EPS)
    mean_all = load_row(mean_4, 0)
    inv_std = load_row(inv_4, 0)
    gain = gain_ref[...]

    wait(others(recv_a), recv_sems.at[1])
    pts = dot_nn(q_t[...], recv_a[...].reshape(REGIONS * CAP, WIDTH))
    unit = (pts - mean_all) * inv_std
    unit_s[...] = unit
    serial[...] = (unit * gain + bias_ref[...]).astype(BF)

    qkv[...] = dot_nn(serial[...], wqkv[...]).astype(BF)
    qs[...] = qkv[:, 0:WIDTH] * jnp.asarray(0.25, BF)
    kt[...] = qkv[:, WIDTH : 2 * WIDTH].T
    query_x[:, 0:128, :] = qs[...].T.reshape(4, 128, PTS)
    value_x[:, 0:HEAD_DIM, :] = qkv[:, 2 * WIDTH : 3 * WIDTH].T.reshape(32, HEAD_DIM, PTS)
    value_x[:, HEAD_DIM : 2 * HEAD_DIM, :] = jnp.ones((32, HEAD_DIM, PTS), BF)

    lane_1 = lax.broadcasted_iota(jnp.int32, (1, 128), 1)

    def head_mask(h):
        return jnp.where(lane_1 // HEAD_DIM == h, 1.0, 0.0).astype(BF)

    def forward(chunk, carry):
        col = pl.multiple_of(chunk * 128, 128)
        keys = qkv[:, pl.ds(WIDTH + col, 128)]
        for h in range(8):
            lhs = jnp.concatenate([keys * head_mask(h), aug_k[...]], axis=1)
            scores = dot_nn(lhs, query_x[chunk])
            e = jnp.exp(scores - jnp.max(scores, axis=0, keepdims=True)).astype(BF)
            es[chunk, :, PTS * h : PTS * (h + 1)] = e
            heads[chunk * 8 + h] = dot_nn(value_x[chunk * 8 + h], e)
        return carry

    lax.fori_loop(0, 4, forward, 0)
    inv_sum = 1.0 / heads[:, HEAD_DIM : HEAD_DIM + 1, :]
    mixed_f[...] = heads[:, 0:HEAD_DIM, :] * inv_sum
    mixed_t[...] = mixed_f[...].reshape(WIDTH, PTS).astype(BF)
    mixed[...] = mixed_t[...].T
    branch = dot_nn(mixed[...], wproj[...]).astype(BF)
    send_c[...] = dot_nn(q_n[...], branch).astype(BF).reshape(REGIONS, CAP, WIDTH)
    each_region(lambda p: send(send_c.at[p], recv_c.at[r], 4, (p, g)))
    recv_c[r] = send_c[r]

    sibling = (r, xx * 2 + 1 - core)

    def to_sibling(at, rows, slot):
        span = pl.ds(at, rows)
        g_core[span, :] = g32[1 - core, span, :].astype(BF)
        remote(g_core.at[span], r_core.at[span], core_send.at[slot], core_recv.at[slot], sibling)

    def to_chips(at, rows, slot):
        span = pl.ds(at, rows)
        wait(r_core.at[span], core_recv.at[slot])
        both = g32[core, span, :] + r_core[span, :].astype(F32)
        for b in range(4):
            s_x[b, span, :] = both[:, 128 * b : 128 * (b + 1)].astype(BF)
        for k in range(1, 4):
            xp = lax.rem(xx + k, 4)
            remote(
                s_x.at[xp, span], r_x.at[xx, span], x_send.at[slot], x_recv.at[slot],
                (r, xp * 2 + core),
            )

    wait(others(recv_b), recv_sems.at[3])
    g_serial = dot_nn(q_t[...], recv_b[...].reshape(REGIONS * CAP, WIDTH)).astype(BF)
    g_serial_t[...] = g_serial.T
    for part in range(4):
        rows = dot_nn(g_serial_t[128 * part : 128 * (part + 1), :], mixed[...])
        for u in range(8):
            at = 4 * CHUNK + part * 64 + (u // 2) * 16
            g32[(u + 1) % 2, at : at + 16, :] = rows[16 * u : 16 * (u + 1), :]
    to_sibling(4 * CHUNK, 256, 4)

    scaled = (
        dot_nn(wproj[...], g_serial_t[...]).reshape(32, HEAD_DIM, PTS) * inv_sum
    ).astype(BF)
    grad_x[:, 0:128, :] = scaled.reshape(4, 128, PTS)
    gm[...] = scaled.reshape(WIDTH, PTS).T
    inner = -jnp.sum(scaled.astype(F32) * mixed_f[...], axis=1, keepdims=True)
    first = inner.astype(BF).astype(F32)
    second = (inner - first).astype(BF).astype(F32)
    third = inner - first - second
    place = lax.broadcasted_iota(jnp.int32, (32, HEAD_DIM, PTS), 1)
    terms = jnp.where(
        place == 0, first, jnp.where(place == 1, second, jnp.where(place == 2, third, 0.0))
    )
    grad_x[:, 128:256, :] = terms.astype(BF).reshape(4, 128, PTS)

    def backward(chunk, carry):
        col = pl.multiple_of(chunk * 128, 128)
        values = qkv[:, pl.ds(2 * WIDTH + col, 128)]
        grads = gm[:, pl.ds(col, 128)]
        queries = qs[:, pl.ds(col, 128)]
        for h in range(8):
            mask = head_mask(h)
            span = slice(PTS * h, PTS * (h + 1))
            chosen = jnp.where(
                (lane_1 // HEAD_DIM == h) & (lane_1 % HEAD_DIM < 3), 1.0, 0.0
            ).astype(BF)
            lhs = jnp.concatenate(
                [values * mask, jnp.broadcast_to(chosen, (PTS, 128))], axis=1
            )
            ds = dot_nn(lhs, grad_x[chunk]).astype(BF) * es[chunk, :, span]
            big_d[:, span] = ds
            stack_g[span, :] = grads * mask
            stack_q[span, :] = queries * mask
            rows = pl.ds(pl.multiple_of(col + HEAD_DIM * h, HEAD_DIM), HEAD_DIM)
            left[HEAD_DIM * h : HEAD_DIM * (h + 1), :] = (dot_nn(kt[rows, :], ds) * 0.25).astype(BF)
        gqkv[:, pl.ds(col, 128)] = left[0:128, :].T
        gk = dot_nn(big_d[...], stack_q[...]).astype(BF)
        gqkv[:, pl.ds(WIDTH + col, 128)] = gk
        left[128:256, :] = gk.T
        gv = dot_nn(es[chunk], stack_g[...]).astype(BF)
        gqkv[:, pl.ds(2 * WIDTH + col, 128)] = gv
        left[256:384, :] = gv.T
        rows = dot_nn(left[...], serial[...])
        base = pl.multiple_of(chunk * CHUNK, 64)
        for p in range(3):
            for u in range(8):
                at = base + p * 64 + (u // 2) * 16
                g32[u % 2, pl.ds(at, 16), :] = rows[128 * p + 16 * u : 128 * p + 16 * (u + 1), :]
        to_sibling(base, CHUNK, chunk)

        @pl.when(chunk == 0)
        def _():
            to_chips(4 * CHUNK, 256, 4)

        @pl.when(chunk > 0)
        def _():
            to_chips(pl.multiple_of((chunk - 1) * CHUNK, 64), CHUNK, chunk - 1)

        return carry

    lax.fori_loop(0, 4, backward, 0)

    grad_in = dot_nt(gqkv[...], wqkv[...]).astype(BF)
    send_d[...] = dot_nn(q_n[...], grad_in).astype(BF).reshape(REGIONS, CAP, WIDTH)
    each_region(lambda p: send(send_d.at[p], recv_d.at[r], 7, (p, g)))
    recv_d[r] = send_d[r]
    to_chips(3 * CHUNK, CHUNK, 3)
    grad_f = grad_in.astype(F32)
    store_rows(gs1, g, 0, jnp.sum(grad_f, axis=0, keepdims=True))
    store_rows(gs1, g, 4, jnp.sum(grad_f * unit_s[...], axis=0, keepdims=True))
    each_group(lambda p: send(gs1.at[g], gs1.at[g], 6, (r, p)))

    wait(others(recv_c), recv_sems.at[4])
    out_ref[...] = dot_nn(p_t[...], recv_c[...].reshape(REGIONS * CAP, WIDTH)).astype(BF)

    wait(others(gs1), recv_sems.at[6])
    gs2[yy] = jnp.sum(gs1[...], axis=0)
    along_y(gs2, 8)

    def gather_chunk(at, rows, slot):
        wait(r_x.at[pl.ds(0, 3), pl.ds(at, rows)], x_recv.at[slot])
        span = slice(at, at + rows)
        mine = pl.ds(pl.multiple_of(xx * 128, 128), 128)
        total = g32[core, span, mine] + r_core[span, mine].astype(F32)
        for k in range(1, 4):
            total = total + r_x[lax.rem(xx + k, 4), span, :].astype(F32)
        return total.astype(BF)

    acc[768:1024, :] = gather_chunk(4 * CHUNK, 256, 4)
    for j in range(4):
        total = gather_chunk(j * CHUNK, CHUNK, j)
        for p in range(3):
            acc[256 * p + 64 * j : 256 * p + 64 * (j + 1), :] = total[64 * p : 64 * (p + 1), :]

    def unit_rows(at):
        return acc[pl.ds(pl.multiple_of(at * 16, 16), 16), :]

    for i in range(16):
        a, b = 2 * i + core, 2 * i + 1 - core
        s_y[a, 0:16, :] = unit_rows(3 * i + core)
        s_y[a, 16:32, :] = unit_rows(3 * i + core + 1)
        s_y[b, 0:16, :] = unit_rows(3 * i + 2 - 2 * core)
        s_y[b, 16:32, :] = unit_rows(48 + i)

    def y_part(at):
        return pl.ds(pl.multiple_of(at * ZS, ZS), ZS)

    for k in range(1, YS):
        yp = lax.rem(yy + k, YS)
        send(s_y.at[y_part(yp)], r_y.at[y_part(yy)], 10, (yp * ZS + zz, g))
    r_y[y_part(yy)] = s_y[y_part(yy)]

    wait(others(gs2), recv_sems.at[8])
    gs3[zz] = jnp.sum(gs2[...], axis=0)
    along_z(gs3, 5)

    wait(r_y.at[pl.ds(0, 3 * ZS)], recv_sems.at[10])
    s_z[...] = jnp.sum(r_y[...].astype(F32).reshape(YS, ZS, 32, 128), axis=0).astype(BF)
    for k in range(1, ZS):
        zp = lax.rem(zz + k, ZS)
        send(s_z.at[zp], r_z.at[zz], 12, (yy * ZS + zp, g))
    r_z[zz] = s_z[zz]

    wait(others(gs3), recv_sems.at[5])
    sums = jnp.sum(gs3[...], axis=0)
    grad_bias = load_row(sums, 0)
    grad_gain = load_row(sums, 4)
    gb_ref[...] = grad_bias
    gg_ref[...] = grad_gain

    wait(others(r_z), recv_sems.at[12])
    fin[core] = jnp.sum(r_z[...].astype(F32), axis=0)
    send(fin.at[core], fin.at[core], 11, sibling)

    wait(others(recv_d), recv_sems.at[7])
    grad_n = dot_nn(p_t[...], recv_d[...].reshape(REGIONS * CAP, WIDTH))
    unit_b = (x_ref[...].astype(F32) - mean_all) * inv_std
    scale = 1.0 / TOTAL
    gp_ref[...] = (
        inv_std
        * (grad_n * gain - gain * grad_bias * scale - unit_b * (gain * grad_gain * scale))
    ).astype(BF)

    wait(fin.at[0], recv_sems.at[11])
    even, odd = fin[r % 2], fin[1 - r % 2]

    def my_lanes(rows):
        return jnp.where(core == 0, rows[:, 0:64], rows[:, 64:128])

    gwq_ref[0:16, :] = my_lanes(even[0:16, :])
    gwq_ref[16:32, :] = my_lanes(odd[0:16, :])
    gwq_ref[32:48, :] = my_lanes(even[16:32, :])
    gwp_ref[...] = my_lanes(odd[16:32, :])

    for buf, stage in (
        (st1, 0), (send_a, 1), (st2, 2), (send_b, 3), (send_c, 4), (gs3, 5), (gs1, 6),
        (send_d, 7), (gs2, 8), (st3, 9), (r_z, 12),
    ):
        wait(others(buf), send_sems.at[stage])
    wait(s_y.at[pl.ds(0, 3 * ZS)], send_sems.at[10])
    wait(fin.at[0], send_sems.at[11])
    for slot, at, rows in [(j, j * CHUNK, CHUNK) for j in range(4)] + [(4, 4 * CHUNK, 256)]:
        wait(g_core.at[pl.ds(at, rows)], core_send.at[slot])
        wait(s_x.at[pl.ds(0, 3), pl.ds(at, rows)], x_send.at[slot])


def deliver(*refs):
    n = len(refs) // 2
    sems = refs[-1]
    copies = [pltpu.make_async_copy(refs[i], refs[n + i], sems.at[i]) for i in range(n)]
    for copy in copies:
        copy.start()
    for copy in copies:
        copy.wait()


def on_device(points, row_slot, pos_slot, patch_ids, bn_gain, bn_bias, w_qkv, w_proj, cotangent):
    vmem = pl.BlockSpec(memory_space=pltpu.VMEM)
    hbm = pl.BlockSpec(memory_space=pltpu.HBM)
    args = tuple(pltpu.with_memory_space_constraint(a, pltpu.HBM) for a in (
        points[0], row_slot, pos_slot, patch_ids[0], bn_gain[None], bn_bias[None],
        w_qkv, w_proj, cotangent[0],
    ))

    def buf(dtype, *shape):
        return pltpu.VMEM(shape, dtype)

    scratch = [buf(a.dtype, *a.shape) for a in args]
    scratch += [pltpu.SemaphoreType.DMA((9,))]
    scratch += [buf(BF, REGIONS, CAP, WIDTH) for _ in range(8)]
    scratch += [buf(F32, n, 8, 128) for n in (GROUPS, YS, ZS, GROUPS, YS, ZS)]
    scratch += [
        buf(BF, PTS, WIDTH),
        buf(BF, WIDTH, PTS),
        buf(BF, PTS, WIDTH),
        buf(BF, PTS, 128),
        buf(BF, 4, 256, PTS),
        buf(BF, 4, 256, PTS),
        buf(F32, PTS, WIDTH),
        buf(BF, PTS, WIDTH),
        buf(BF, PTS, 3 * WIDTH),
        buf(BF, PTS, WIDTH),
        buf(BF, WIDTH, PTS),
        buf(BF, 32, 2 * HEAD_DIM, PTS),
        buf(BF, 4, PTS, 8 * PTS),
        buf(F32, 32, 2 * HEAD_DIM, PTS),
        buf(F32, 32, HEAD_DIM, PTS),
        buf(BF, WIDTH, PTS),
        buf(BF, PTS, WIDTH),
        buf(BF, WIDTH, PTS),
        buf(BF, PTS, WIDTH),
        buf(BF, PTS, 8 * PTS),
        buf(BF, 8 * PTS, 128),
        buf(BF, 8 * PTS, 128),
        buf(BF, PTS, 3 * WIDTH),
        buf(BF, 384, PTS),
        buf(F32, 2, 1024, WIDTH),
        buf(BF, 1024, WIDTH),
        buf(BF, 1024, WIDTH),
        buf(BF, 4, 1024, 128),
        buf(BF, 4, 1024, 128),
        buf(BF, 1024, 128),
        buf(BF, REGIONS, 32, 128),
        buf(BF, REGIONS, 32, 128),
        buf(BF, ZS, 32, 128),
        buf(BF, ZS, 32, 128),
        buf(F32, 2, 32, 128),
    ]
    scratch += [pltpu.SemaphoreType.DMA((n,)) for n in (13, 13, 5, 5, 5, 5)]
    shapes = [
        jax.ShapeDtypeStruct((PTS, WIDTH), BF),
        jax.ShapeDtypeStruct((PTS, WIDTH), BF),
        jax.ShapeDtypeStruct((48, 64), F32),
        jax.ShapeDtypeStruct((16, 64), F32),
        jax.ShapeDtypeStruct((1, WIDTH), F32),
        jax.ShapeDtypeStruct((1, WIDTH), F32),
    ]
    results = pl.pallas_call(
        kernel,
        out_shape=shapes,
        in_specs=[hbm] * 9,
        out_specs=[vmem] * 6,
        scratch_shapes=scratch,
        compiler_params=pltpu.CompilerParams(
            collective_id=0, has_side_effects=True, vmem_limit_bytes=52 * 1024 * 1024
        ),
    )(*args)
    output, grad_points, grad_qkv, grad_proj, grad_gain, grad_bias = pl.pallas_call(
        deliver,
        out_shape=shapes,
        in_specs=[vmem] * 6,
        out_specs=[hbm] * 6,
        scratch_shapes=[pltpu.SemaphoreType.DMA((6,))],
    )(*results)
    return output[None], grad_points[None], grad_qkv.T, grad_proj.T, grad_gain[0], grad_bias[0]


def solution(mesh):
    placed = (
        P("group", "region", None),
        P("group", "region"),
        P("group", "region"),
        P("group", "region", None),
        P(),
        P(),
        P(),
        P(),
        P("group", "region", None),
    )
    return jax.shard_map(
        on_device,
        mesh=mesh,
        in_specs=placed,
        out_specs=(
            P("group", "region", None),
            P("group", "region", None),
            P("group", "region"),
            P("group", "region"),
            P(),
            P(),
        ),
        check_vma=False,
    )
```

time: 95.7 us -> 79.3 us (0.83)
  Pallas kernels: 84.5 us -> 74.8 us
  local copies, waits for them, and re-layouts: 10.2 us -> 3.72 us
    pallas_call x1 -> x2, Pallas kernels: 84.5 us -> 74.8 us  [the longest x1 72.9 us: on_device(): pl.pallas_call(kernel, out_shape=shapes, in_specs=[hbm] * 9, out_specs=[v...]
    unnamed x22 -> x12, local copies, waits for them, and re-layouts: 10.2 us -> 3.72 us
where the time goes in v2:
time: 79.3 us; the launch traced here: 79.2 us
  Pallas kernels  74.8 us (94%)
  local copies, waits for them, and re-layouts  3.72 us (5%)
    pallas_call x1, Pallas kernels, on_device(): pl.pallas_call(kernel, out_shape=shapes, in_specs=[hbm] * 9, out_specs=[v...  72.9 us
    unnamed x12, local copies, waits for them, and re-layouts  3.72 us
    pallas_call x1, Pallas kernels, on_device(): pl.pallas_call(deliver, out_shape=shapes, in_specs=[vmem] * 6, out_specs=...  1.9 us

profile of v2, /device:TPU:1, one launch (start us, length us, event | category | flops | bytes accessed | tf_op | source)
XLA Modules:
  0.0 79.2 jit_solution(11685336939787794777)
XLA Ops:
  0.6 72.9 %shard_map.136 = (bf16[256,512]{1,0:T(8,128)(2,1)S(1)}, bf16[256,512]{1,0:T(8,128)(2,1)S(1)}, f32[48,64]{1,0:T(8,128)S(1)}, f32[16,64]{1,0:T(8,128)S(1)}, f32[1,512]{1,0:T(1,128)S(1)}, /*index=5*/f32[1,512]{1,0:T(1,128)S(1)}) custom-call(bf16[256,512]{1,0:T(8,128)(2,1)} %bitcast.11, s32[1,256]{1,0:T(1,128)} %rs_hbm.1, s32[1,256]{1,0:T(1,128)} %ps_hbm.1, ...), custom_call_target="tpu_custom_call" | custom-call | tf_op jit(solution)/shard_map/pallas_call | solution.py:497
  73.6 0.0 copy-start
  73.6 0.7 copy-done
  74.3 0.0 copy-start.1
  74.3 0.7 copy-done.1
  75.0 0.0 copy-start.2
  75.0 0.6 copy-done.2
  75.6 0.0 copy-start.3
  75.6 0.6 copy-done.3
  76.2 0.0 copy-start.4
  76.2 0.6 copy-done.4
  76.7 0.0 copy-start.5
  76.7 0.6 copy-done.5
  77.3 1.9 %shard_map.137 = (bf16[256,512]{1,0:T(8,128)(2,1)}, bf16[256,512]{1,0:T(8,128)(2,1)}, f32[48,64]{1,0:T(8,128)}, f32[16,64]{1,0:T(8,128)}, f32[1,512]{1,0:T(1,128)}, /*index=5*/f32[1,512]{1,0:T(1,128)}) custom-call(bf16[256,512]{1,0:T(8,128)(2,1)} %copy-done, bf16[256,512]{1,0:T(8,128)(2,1)} %copy-done.1, f32[48,64]{1,0:T(8,128)} %copy-done.2, ...), custom_call_target="tpu_custom_call" | custom-call | tf_op jit(solution)/shard_map/pallas_call | solution.py:507
Async XLA Ops:
  73.6 0.7 copy-start
  74.3 0.7 copy-start.1
  75.0 0.6 copy-start.2
  75.6 0.6 copy-start.3
  76.2 0.6 copy-start.4
  76.7 0.6 copy-start.5

commit v3 on v2

--- a/solution.py
+++ b/solution.py
@@ -62,7 +62,7 @@
     send_a, recv_a, send_b, recv_b, send_c, recv_c, send_d, recv_d,
     st1, st2, st3, gs1, gs2, gs3,
     p_t, q_n, q_t, aug_k, query_x, grad_x,
-    unit_s, serial, qkv, qs, kt, value_x, es, heads, mixed_f, mixed_t, mixed,
+    unit_s, serial, qkv, qs, kt, value_x, score, es, heads, mixed_f, mixed_t, mixed,
     g_serial_t, gm, big_d, stack_g, stack_q, gqkv, left,
     g32, g_core, r_core, s_x, r_x, acc, s_y, r_y, s_z, r_z, fin,
     send_sems, recv_sems, core_send, core_recv, x_send, x_recv,
@@ -211,9 +211,12 @@
         keys = qkv[:, pl.ds(WIDTH + col, 128)]
         for h in range(8):
             lhs = jnp.concatenate([keys * head_mask(h), aug_k[...]], axis=1)
-            scores = dot_nn(lhs, query_x[chunk])
-            e = jnp.exp(scores - jnp.max(scores, axis=0, keepdims=True)).astype(BF)
-            es[chunk, :, PTS * h : PTS * (h + 1)] = e
+            score[h] = dot_nn(lhs, query_x[chunk])
+        for h in range(8):
+            top = jnp.max(score[h], axis=0, keepdims=True)
+            es[chunk, :, PTS * h : PTS * (h + 1)] = jnp.exp(score[h] - top).astype(BF)
+        for h in range(8):
+            e = es[chunk, :, PTS * h : PTS * (h + 1)]
             heads[chunk * 8 + h] = dot_nn(value_x[chunk * 8 + h], e)
         return carry
 
@@ -277,21 +280,24 @@
         values = qkv[:, pl.ds(2 * WIDTH + col, 128)]
         grads = gm[:, pl.ds(col, 128)]
         queries = qs[:, pl.ds(col, 128)]
+        spans = [slice(PTS * h, PTS * (h + 1)) for h in range(8)]
         for h in range(8):
-            mask = head_mask(h)
-            span = slice(PTS * h, PTS * (h + 1))
+            stack_g[spans[h], :] = grads * head_mask(h)
+            stack_q[spans[h], :] = queries * head_mask(h)
+        for h in range(8):
             chosen = jnp.where(
                 (lane_1 // HEAD_DIM == h) & (lane_1 % HEAD_DIM < 3), 1.0, 0.0
             ).astype(BF)
             lhs = jnp.concatenate(
-                [values * mask, jnp.broadcast_to(chosen, (PTS, 128))], axis=1
+                [values * head_mask(h), jnp.broadcast_to(chosen, (PTS, 128))], axis=1
             )
-            ds = dot_nn(lhs, grad_x[chunk]).astype(BF) * es[chunk, :, span]
-            big_d[:, span] = ds
-            stack_g[span, :] = grads * mask
-            stack_q[span, :] = queries * mask
+            ds = dot_nn(lhs, grad_x[chunk]).astype(BF) * es[chunk, :, spans[h]]
+            big_d[:, spans[h]] = ds
+        for h in range(8):
             rows = pl.ds(pl.multiple_of(col + HEAD_DIM * h, HEAD_DIM), HEAD_DIM)
-            left[HEAD_DIM * h : HEAD_DIM * (h + 1), :] = (dot_nn(kt[rows, :], ds) * 0.25).astype(BF)
+            left[HEAD_DIM * h : HEAD_DIM * (h + 1), :] = (
+                dot_nn(kt[rows, :], big_d[:, spans[h]]) * 0.25
+            ).astype(BF)
         gqkv[:, pl.ds(col, 128)] = left[0:128, :].T
         gk = dot_nn(big_d[...], stack_q[...]).astype(BF)
         gqkv[:, pl.ds(WIDTH + col, 128)] = gk
@@ -461,6 +467,7 @@
         buf(BF, PTS, WIDTH),
         buf(BF, WIDTH, PTS),
         buf(BF, 32, 2 * HEAD_DIM, PTS),
+        buf(F32, 8, PTS, PTS),
         buf(BF, 4, PTS, 8 * PTS),
         buf(F32, 32, 2 * HEAD_DIM, PTS),
         buf(F32, 32, HEAD_DIM, PTS),
@@ -507,9 +514,10 @@
     output, grad_points, grad_qkv, grad_proj, grad_gain, grad_bias = pl.pallas_call(
         deliver,
         out_shape=shapes,
-        in_specs=[vmem] * 6,
+        in_specs=[pl.BlockSpec(memory_space=pl.ANY)] * 6,
         out_specs=[hbm] * 6,
         scratch_shapes=[pltpu.SemaphoreType.DMA((6,))],
+        compiler_params=pltpu.CompilerParams(vmem_limit_bytes=4 * 1024 * 1024),
     )(*results)
     return output[None], grad_points[None], grad_qkv.T, grad_proj.T, grad_gain[0], grad_bias[0]
 

time: 79.3 us -> 71.6 us (0.903)
  Pallas kernels: 74.8 us -> 70.8 us
  local copies, waits for them, and re-layouts: 3.72 us -> 0 us
    unnamed x12 -> x0, local copies, waits for them, and re-layouts: 3.72 us -> none
    pallas_call x1, Pallas kernels: 72.9 us -> 70 us  [on_device(): pl.pallas_call(kernel, out_shape=shapes, in_specs=[hbm] * 9, out_specs=[v...]
    pallas_call x1, Pallas kernels: 1.9 us -> 0.85 us  [on_device(): pl.pallas_call(deliver, out_shape=shapes, in_specs=[pl.BlockSpec(memory_s...]
where the time goes in v3:
time: 71.6 us; the launch traced here: 71.5 us
  Pallas kernels  70.8 us (99%)
    pallas_call x1, Pallas kernels, on_device(): pl.pallas_call(kernel, out_shape=shapes, in_specs=[hbm] * 9, out_specs=[v...  70 us

profile of v3, /device:TPU:1, one launch (start us, length us, event | category | flops | bytes accessed | tf_op | source)
XLA Modules:
  0.0 71.5 jit_solution(8340051298328237313)
XLA Ops:
  0.6 70.0 %shard_map.136 = (bf16[256,512]{1,0:T(8,128)(2,1)S(1)}, bf16[256,512]{1,0:T(8,128)(2,1)S(1)}, f32[48,64]{1,0:T(8,128)S(1)}, f32[16,64]{1,0:T(8,128)S(1)}, f32[1,512]{1,0:T(1,128)S(1)}, /*index=5*/f32[1,512]{1,0:T(1,128)S(1)}) custom-call(bf16[256,512]{1,0:T(8,128)(2,1)} %bitcast.11, s32[1,256]{1,0:T(1,128)} %rs_hbm.1, s32[1,256]{1,0:T(1,128)} %ps_hbm.1, ...), custom_call_target="tpu_custom_call" | custom-call | tf_op jit(solution)/shard_map/pallas_call | solution.py:504
  70.6 0.9 %shard_map.137 = (bf16[256,512]{1,0:T(8,128)(2,1)}, bf16[256,512]{1,0:T(8,128)(2,1)}, f32[48,64]{1,0:T(8,128)}, f32[16,64]{1,0:T(8,128)}, f32[1,512]{1,0:T(1,128)}, /*index=5*/f32[1,512]{1,0:T(1,128)}) custom-call(bf16[256,512]{1,0:T(8,128)(2,1)S(1)} %get-tuple-element.18.refs_0_, bf16[256,512]{1,0:T(8,128)(2,1)S(1)} %get-tuple-element.19.refs_1_, ...), custom_call_target="tpu_custom_call" | custom-call | tf_op jit(solution)/shard_map/pallas_call | solution.py:514

commit v4 on v3

--- a/solution.py
+++ b/solution.py
@@ -1,5 +1,3 @@
-import functools
-
 import jax
 import jax.numpy as jnp
 from jax import lax
@@ -64,20 +62,20 @@
     p_t, q_n, q_t, aug_k, query_x, grad_x,
     unit_s, serial, qkv, qs, kt, value_x, score, es, heads, mixed_f, mixed_t, mixed,
     g_serial_t, gm, big_d, stack_g, stack_q, gqkv, left,
-    g32, g_core, r_core, s_x, r_x, acc, s_y, r_y, s_z, r_z, fin,
-    send_sems, recv_sems, core_send, core_recv, x_send, x_recv,
+    right_s, right_m, own, g_core, r_core, s_x, r_x, s_y, r_y, s_z, r_z,
+    send_sems, recv_sems, core_send, core_recv, x_send, x_recv, y_send, y_recv,
 ):
     r = lax.axis_index("region")
     g = lax.axis_index("group")
     xx, core = g // 2, g % 2
     yy, zz = r // ZS, r % ZS
 
-    def each_region(act):
+    def each_region(act, first=1, end=REGIONS):
         def body(k, carry):
             act(lax.rem(r + k, REGIONS))
             return carry
 
-        lax.fori_loop(1, REGIONS, body, 0)
+        lax.fori_loop(first, end, body, 0)
 
     def each_group(act):
         def body(k, carry):
@@ -227,20 +225,34 @@
     mixed[...] = mixed_t[...].T
     branch = dot_nn(mixed[...], wproj[...]).astype(BF)
     send_c[...] = dot_nn(q_n[...], branch).astype(BF).reshape(REGIONS, CAP, WIDTH)
-    each_region(lambda p: send(send_c.at[p], recv_c.at[r], 4, (p, g)))
-    recv_c[r] = send_c[r]
 
     sibling = (r, xx * 2 + 1 - core)
-
-    def to_sibling(at, rows, slot):
+    low_lanes = lax.broadcasted_iota(jnp.int32, (1, WIDTH), 1) % 128 < 64
+
+    def packed(ref, source):
+        rows = source.astype(F32)
+        none = jnp.zeros_like(rows)
+        for c, turn in ((0, 64), (1, WIDTH - 64)):
+            turned = pltpu.roll(rows, turn, 1)
+            first, second = (rows, turned) if c == 0 else (turned, rows)
+            ref[c, 0:PTS, :] = jnp.where(low_lanes, first, none).astype(BF)
+            ref[c, PTS : 2 * PTS, :] = jnp.where(low_lanes, none, second).astype(BF)
+
+    def to_sibling(units, right, at, rows, slot):
         span = pl.ds(at, rows)
-        g_core[span, :] = g32[1 - core, span, :].astype(BF)
+        own[span, :] = dot_nn(units, right[core])
+        g_core[span, :] = dot_nn(units, right[1 - core]).astype(BF)
         remote(g_core.at[span], r_core.at[span], core_send.at[slot], core_recv.at[slot], sibling)
+
+    def unit_pairs(rows, swap):
+        by_unit = rows.reshape(rows.shape[0] // 32, 2, 16, PTS)
+        halves = [by_unit[:, k].reshape(rows.shape[0] // 2, PTS) for k in range(2)]
+        return jnp.concatenate(halves[::-1] if swap else halves, axis=1)
 
     def to_chips(at, rows, slot):
         span = pl.ds(at, rows)
         wait(r_core.at[span], core_recv.at[slot])
-        both = g32[core, span, :] + r_core[span, :].astype(F32)
+        both = own[span, :] + r_core[span, :].astype(F32)
         for b in range(4):
             s_x[b, span, :] = both[:, 128 * b : 128 * (b + 1)].astype(BF)
         for k in range(1, 4):
@@ -250,15 +262,15 @@
                 (r, xp * 2 + core),
             )
 
+    packed(right_s, serial[...])
+    packed(right_m, mixed[...])
+
     wait(others(recv_b), recv_sems.at[3])
+    each_region(lambda p: send(send_c.at[p], recv_c.at[r], 4, (p, g)))
+    recv_c[r] = send_c[r]
     g_serial = dot_nn(q_t[...], recv_b[...].reshape(REGIONS * CAP, WIDTH)).astype(BF)
     g_serial_t[...] = g_serial.T
-    for part in range(4):
-        rows = dot_nn(g_serial_t[128 * part : 128 * (part + 1), :], mixed[...])
-        for u in range(8):
-            at = 4 * CHUNK + part * 64 + (u // 2) * 16
-            g32[(u + 1) % 2, at : at + 16, :] = rows[16 * u : 16 * (u + 1), :]
-    to_sibling(4 * CHUNK, 256, 4)
+    to_sibling(unit_pairs(g_serial_t[...], True), right_m, 4 * CHUNK, 256, 4)
 
     scaled = (
         dot_nn(wproj[...], g_serial_t[...]).reshape(32, HEAD_DIM, PTS) * inv_sum
@@ -305,13 +317,8 @@
         gv = dot_nn(es[chunk], stack_g[...]).astype(BF)
         gqkv[:, pl.ds(2 * WIDTH + col, 128)] = gv
         left[256:384, :] = gv.T
-        rows = dot_nn(left[...], serial[...])
         base = pl.multiple_of(chunk * CHUNK, 64)
-        for p in range(3):
-            for u in range(8):
-                at = base + p * 64 + (u // 2) * 16
-                g32[u % 2, pl.ds(at, 16), :] = rows[128 * p + 16 * u : 128 * p + 16 * (u + 1), :]
-        to_sibling(base, CHUNK, chunk)
+        to_sibling(unit_pairs(left[...], False), right_s, base, CHUNK, chunk)
 
         @pl.when(chunk == 0)
         def _():
@@ -335,55 +342,72 @@
     store_rows(gs1, g, 4, jnp.sum(grad_f * unit_s[...], axis=0, keepdims=True))
     each_group(lambda p: send(gs1.at[g], gs1.at[g], 6, (r, p)))
 
-    wait(others(recv_c), recv_sems.at[4])
-    out_ref[...] = dot_nn(p_t[...], recv_c[...].reshape(REGIONS * CAP, WIDTH)).astype(BF)
+    def gather_chips(at, rows, slot):
+        wait(r_x.at[pl.ds(0, 3), pl.ds(at, rows)], x_recv.at[slot])
+        span = slice(at, at + rows)
+        mine = pl.ds(pl.multiple_of(xx * 128, 128), 128)
+        total = own[span, mine] + r_core[span, mine].astype(F32)
+        for k in range(1, 4):
+            total = total + r_x[lax.rem(xx + k, 4), span, :].astype(F32)
+        return total.astype(BF)
+
+    def to_y(at, owner, row, slot):
+        remote(
+            s_y.at[pl.ds(at, 64)], r_y.at[yy, pl.ds(row, 64)], y_send.at[0], y_recv.at[slot],
+            (owner * ZS + zz, g),
+        )
+
+    def chunk_to_y(j):
+        total = gather_chips(j * CHUNK, CHUNK, j)
+        for p in range(3):
+            b = p * 4 + j
+            s_y[64 * b : 64 * (b + 1), :] = total[64 * p : 64 * (p + 1), :]
+
+            @pl.when(yy != b // 3)
+            def _():
+                to_y(64 * b, b // 3, 64 * (b % 3), b % 3)
+
+    s_y[768:1024, :] = gather_chips(4 * CHUNK, 256, 4)
+    for k in range(1, YS):
+        yp = lax.rem(yy + k, YS)
+        to_y(pl.multiple_of(768 + yp * 64, 64), yp, 192, 3)
+    chunk_to_y(0)
 
     wait(others(gs1), recv_sems.at[6])
     gs2[yy] = jnp.sum(gs1[...], axis=0)
     along_y(gs2, 8)
-
-    def gather_chunk(at, rows, slot):
-        wait(r_x.at[pl.ds(0, 3), pl.ds(at, rows)], x_recv.at[slot])
-        span = slice(at, at + rows)
-        mine = pl.ds(pl.multiple_of(xx * 128, 128), 128)
-        total = g32[core, span, mine] + r_core[span, mine].astype(F32)
-        for k in range(1, 4):
-            total = total + r_x[lax.rem(xx + k, 4), span, :].astype(F32)
-        return total.astype(BF)
-
-    acc[768:1024, :] = gather_chunk(4 * CHUNK, 256, 4)
-    for j in range(4):
-        total = gather_chunk(j * CHUNK, CHUNK, j)
-        for p in range(3):
-            acc[256 * p + 64 * j : 256 * p + 64 * (j + 1), :] = total[64 * p : 64 * (p + 1), :]
-
-    def unit_rows(at):
-        return acc[pl.ds(pl.multiple_of(at * 16, 16), 16), :]
-
-    for i in range(16):
-        a, b = 2 * i + core, 2 * i + 1 - core
-        s_y[a, 0:16, :] = unit_rows(3 * i + core)
-        s_y[a, 16:32, :] = unit_rows(3 * i + core + 1)
-        s_y[b, 0:16, :] = unit_rows(3 * i + 2 - 2 * core)
-        s_y[b, 16:32, :] = unit_rows(48 + i)
-
-    def y_part(at):
-        return pl.ds(pl.multiple_of(at * ZS, ZS), ZS)
-
-    for k in range(1, YS):
-        yp = lax.rem(yy + k, YS)
-        send(s_y.at[y_part(yp)], r_y.at[y_part(yy)], 10, (yp * ZS + zz, g))
-    r_y[y_part(yy)] = s_y[y_part(yy)]
+    chunk_to_y(1)
+
+    wait(others(recv_c), recv_sems.at[4])
+    out_ref[...] = dot_nn(p_t[...], recv_c[...].reshape(REGIONS * CAP, WIDTH)).astype(BF)
 
     wait(others(gs2), recv_sems.at[8])
     gs3[zz] = jnp.sum(gs2[...], axis=0)
     along_z(gs3, 5)
 
-    wait(r_y.at[pl.ds(0, 3 * ZS)], recv_sems.at[10])
-    s_z[...] = jnp.sum(r_y[...].astype(F32).reshape(YS, ZS, 32, 128), axis=0).astype(BF)
+    chunk_to_y(2)
+    chunk_to_y(3)
+    for m in range(3):
+        at = pl.multiple_of((yy * 3 + m) * 64, 64)
+        r_y[yy, 64 * m : 64 * (m + 1), :] = s_y[pl.ds(at, 64), :]
+    r_y[yy, 192:256, :] = s_y[pl.ds(pl.multiple_of(768 + yy * 64, 64), 64), :]
+    for slot in range(4):
+        wait(r_y.at[pl.ds(0, 3), pl.ds(64 * slot, 64)], y_recv.at[slot])
+    over_y = jnp.sum(r_y[...].astype(F32), axis=0).astype(BF)
+    low = low_lanes[:, 0:128]
+
+    def rows_of(unit):
+        return over_y[16 * unit : 16 * (unit + 1), :]
+
+    for z in range(ZS):
+        half = z // 2
+        middle, proj = rows_of(3 * half + 1).astype(F32), rows_of(12 + half).astype(F32)
+        s_z[z, 0:16, :] = rows_of(3 * half + 2 * (z % 2))
+        mixed_rows = jnp.where(low, proj, middle) if z % 2 else jnp.where(low, middle, proj)
+        s_z[z, 16:32, :] = mixed_rows.astype(BF)
     for k in range(1, ZS):
         zp = lax.rem(zz + k, ZS)
-        send(s_z.at[zp], r_z.at[zz], 12, (yy * ZS + zp, g))
+        send(s_z.at[zp], r_z.at[zz], 10, (yy * ZS + zp, g))
     r_z[zz] = s_z[zz]
 
     wait(others(gs3), recv_sems.at[5])
@@ -392,10 +416,6 @@
     grad_gain = load_row(sums, 4)
     gb_ref[...] = grad_bias
     gg_ref[...] = grad_gain
-
-    wait(others(r_z), recv_sems.at[12])
-    fin[core] = jnp.sum(r_z[...].astype(F32), axis=0)
-    send(fin.at[core], fin.at[core], 11, sibling)
 
     wait(others(recv_d), recv_sems.at[7])
     grad_n = dot_nn(p_t[...], recv_d[...].reshape(REGIONS * CAP, WIDTH))
@@ -406,24 +426,22 @@
         * (grad_n * gain - gain * grad_bias * scale - unit_b * (gain * grad_gain * scale))
     ).astype(BF)
 
-    wait(fin.at[0], recv_sems.at[11])
-    even, odd = fin[r % 2], fin[1 - r % 2]
-
-    def my_lanes(rows):
-        return jnp.where(core == 0, rows[:, 0:64], rows[:, 64:128])
-
-    gwq_ref[0:16, :] = my_lanes(even[0:16, :])
-    gwq_ref[16:32, :] = my_lanes(odd[0:16, :])
-    gwq_ref[32:48, :] = my_lanes(even[16:32, :])
-    gwp_ref[...] = my_lanes(odd[16:32, :])
+    wait(others(r_z), recv_sems.at[10])
+    final = jnp.sum(r_z[...].astype(F32), axis=0)
+    even = zz % 2 == 0
+    a, b = final[0:16, 0:64], final[0:16, 64:128]
+    c, d = final[16:32, 0:64], final[16:32, 64:128]
+    gwq_ref[0:16, :] = jnp.where(even, a, d)
+    gwq_ref[16:32, :] = jnp.where(even, b, a)
+    gwq_ref[32:48, :] = jnp.where(even, c, b)
+    gwp_ref[...] = jnp.where(even, d, c)
 
     for buf, stage in (
         (st1, 0), (send_a, 1), (st2, 2), (send_b, 3), (send_c, 4), (gs3, 5), (gs1, 6),
-        (send_d, 7), (gs2, 8), (st3, 9), (r_z, 12),
+        (send_d, 7), (gs2, 8), (st3, 9), (r_z, 10),
     ):
         wait(others(buf), send_sems.at[stage])
-    wait(s_y.at[pl.ds(0, 3 * ZS)], send_sems.at[10])
-    wait(fin.at[0], send_sems.at[11])
+    wait(s_y.at[pl.ds(0, 768)], y_send.at[0])
     for slot, at, rows in [(j, j * CHUNK, CHUNK) for j in range(4)] + [(4, 4 * CHUNK, 256)]:
         wait(g_core.at[pl.ds(at, rows)], core_send.at[slot])
         wait(s_x.at[pl.ds(0, 3), pl.ds(at, rows)], x_send.at[slot])
@@ -480,19 +498,19 @@
         buf(BF, 8 * PTS, 128),
         buf(BF, PTS, 3 * WIDTH),
         buf(BF, 384, PTS),
-        buf(F32, 2, 1024, WIDTH),
+        buf(BF, 2, 2 * PTS, WIDTH),
+        buf(BF, 2, 2 * PTS, WIDTH),
+        buf(F32, 1024, WIDTH),
         buf(BF, 1024, WIDTH),
         buf(BF, 1024, WIDTH),
         buf(BF, 4, 1024, 128),
         buf(BF, 4, 1024, 128),
         buf(BF, 1024, 128),
-        buf(BF, REGIONS, 32, 128),
-        buf(BF, REGIONS, 32, 128),
+        buf(BF, YS, 256, 128),
         buf(BF, ZS, 32, 128),
         buf(BF, ZS, 32, 128),
-        buf(F32, 2, 32, 128),
     ]
-    scratch += [pltpu.SemaphoreType.DMA((n,)) for n in (13, 13, 5, 5, 5, 5)]
+    scratch += [pltpu.SemaphoreType.DMA((n,)) for n in (11, 11, 5, 5, 5, 5, 1, 4)]
     shapes = [
         jax.ShapeDtypeStruct((PTS, WIDTH), BF),
         jax.ShapeDtypeStruct((PTS, WIDTH), BF),

time: 71.6 us -> 69 us (0.964)
  Pallas kernels: 70.8 us -> 67.8 us
    pallas_call x1, Pallas kernels: 70 us -> 66.9 us  [on_device(): pl.pallas_call(kernel, out_shape=shapes, in_specs=[hbm] * 9, out_specs=[v...]
where the time goes in v4:
time: 69 us; the launch traced here: 68.4 us
  Pallas kernels  67.8 us (98%)
    pallas_call x1, Pallas kernels, on_device(): pl.pallas_call(kernel, out_shape=shapes, in_specs=[hbm] * 9, out_specs=[v...  66.9 us

profile of v4, /device:TPU:1, one launch (start us, length us, event | category | flops | bytes accessed | tf_op | source)
XLA Modules:
  0.0 68.4 jit_solution(6650384411090191022)
XLA Ops:
  0.6 66.9 %shard_map.136 = (bf16[256,512]{1,0:T(8,128)(2,1)S(1)}, bf16[256,512]{1,0:T(8,128)(2,1)S(1)}, f32[48,64]{1,0:T(8,128)S(1)}, f32[16,64]{1,0:T(8,128)S(1)}, f32[1,512]{1,0:T(1,128)S(1)}, /*index=5*/f32[1,512]{1,0:T(1,128)S(1)}) custom-call(bf16[256,512]{1,0:T(8,128)(2,1)} %bitcast.11, s32[1,256]{1,0:T(1,128)} %rs_hbm.1, s32[1,256]{1,0:T(1,128)} %ps_hbm.1, ...), custom_call_target="tpu_custom_call" | custom-call | tf_op jit(solution)/shard_map/pallas_call | solution.py:522
  67.5 0.9 %shard_map.137 = (bf16[256,512]{1,0:T(8,128)(2,1)}, bf16[256,512]{1,0:T(8,128)(2,1)}, f32[48,64]{1,0:T(8,128)}, f32[16,64]{1,0:T(8,128)}, f32[1,512]{1,0:T(1,128)}, /*index=5*/f32[1,512]{1,0:T(1,128)}) custom-call(bf16[256,512]{1,0:T(8,128)(2,1)S(1)} %get-tuple-element.18.refs_0_, bf16[256,512]{1,0:T(8,128)(2,1)S(1)} %get-tuple-element.19.refs_1_, ...), custom_call_target="tpu_custom_call" | custom-call | tf_op jit(solution)/shard_map/pallas_call | solution.py:532

commit v5 on v4

--- a/solution.py
+++ b/solution.py
@@ -373,19 +373,16 @@
         to_y(pl.multiple_of(768 + yp * 64, 64), yp, 192, 3)
     chunk_to_y(0)
 
+    chunk_to_y(1)
+
+    wait(others(recv_c), recv_sems.at[4])
+    out_ref[...] = dot_nn(p_t[...], recv_c[...].reshape(REGIONS * CAP, WIDTH)).astype(BF)
+
+
+    chunk_to_y(2)
     wait(others(gs1), recv_sems.at[6])
     gs2[yy] = jnp.sum(gs1[...], axis=0)
     along_y(gs2, 8)
-    chunk_to_y(1)
-
-    wait(others(recv_c), recv_sems.at[4])
-    out_ref[...] = dot_nn(p_t[...], recv_c[...].reshape(REGIONS * CAP, WIDTH)).astype(BF)
-
-    wait(others(gs2), recv_sems.at[8])
-    gs3[zz] = jnp.sum(gs2[...], axis=0)
-    along_z(gs3, 5)
-
-    chunk_to_y(2)
     chunk_to_y(3)
     for m in range(3):
         at = pl.multiple_of((yy * 3 + m) * 64, 64)
@@ -409,6 +406,14 @@
         zp = lax.rem(zz + k, ZS)
         send(s_z.at[zp], r_z.at[zz], 10, (yy * ZS + zp, g))
     r_z[zz] = s_z[zz]
+    wait(others(gs2), recv_sems.at[8])
+    gs3[zz] = jnp.sum(gs2[...], axis=0)
+    along_z(gs3, 5)
+
+    wait(others(recv_d), recv_sems.at[7])
+    grad_n = dot_nn(p_t[...], recv_d[...].reshape(REGIONS * CAP, WIDTH))
+    scaled_n = grad_n * (inv_std * gain)
+    unit_b = (x_ref[...].astype(F32) - mean_all) * inv_std
 
     wait(others(gs3), recv_sems.at[5])
     sums = jnp.sum(gs3[...], axis=0)
@@ -416,15 +421,8 @@
     grad_gain = load_row(sums, 4)
     gb_ref[...] = grad_bias
     gg_ref[...] = grad_gain
-
-    wait(others(recv_d), recv_sems.at[7])
-    grad_n = dot_nn(p_t[...], recv_d[...].reshape(REGIONS * CAP, WIDTH))
-    unit_b = (x_ref[...].astype(F32) - mean_all) * inv_std
-    scale = 1.0 / TOTAL
-    gp_ref[...] = (
-        inv_std
-        * (grad_n * gain - gain * grad_bias * scale - unit_b * (gain * grad_gain * scale))
-    ).astype(BF)
+    scale = inv_std * gain * (1.0 / TOTAL)
+    gp_ref[...] = (scaled_n - scale * grad_bias - unit_b * (scale * grad_gain)).astype(BF)
 
     wait(others(r_z), recv_sems.at[10])
     final = jnp.sum(r_z[...].astype(F32), axis=0)

time: 69 us -> 66.6 us (0.965)
  Pallas kernels: 67.8 us -> 65.8 us
    pallas_call x1, Pallas kernels: 66.9 us -> 64.9 us  [on_device(): pl.pallas_call(kernel, out_shape=shapes, in_specs=[hbm] * 9, out_specs=[v...]
where the time goes in v5:
time: 66.6 us; the launch traced here: 66.4 us
  Pallas kernels  65.8 us (99%)
    pallas_call x1, Pallas kernels, on_device(): pl.pallas_call(kernel, out_shape=shapes, in_specs=[hbm] * 9, out_specs=[v...  64.9 us

profile of v5, /device:TPU:1, one launch (start us, length us, event | category | flops | bytes accessed | tf_op | source)
XLA Modules:
  0.0 66.4 jit_solution(16877597771461054021)
XLA Ops:
  0.6 64.9 %shard_map.136 = (bf16[256,512]{1,0:T(8,128)(2,1)S(1)}, bf16[256,512]{1,0:T(8,128)(2,1)S(1)}, f32[48,64]{1,0:T(8,128)S(1)}, f32[16,64]{1,0:T(8,128)S(1)}, f32[1,512]{1,0:T(1,128)S(1)}, /*index=5*/f32[1,512]{1,0:T(1,128)S(1)}) custom-call(bf16[256,512]{1,0:T(8,128)(2,1)} %bitcast.11, s32[1,256]{1,0:T(1,128)} %rs_hbm.1, s32[1,256]{1,0:T(1,128)} %ps_hbm.1, ...), custom_call_target="tpu_custom_call" | custom-call | tf_op jit(solution)/shard_map/pallas_call | solution.py:520
  65.6 0.9 %shard_map.137 = (bf16[256,512]{1,0:T(8,128)(2,1)}, bf16[256,512]{1,0:T(8,128)(2,1)}, f32[48,64]{1,0:T(8,128)}, f32[16,64]{1,0:T(8,128)}, f32[1,512]{1,0:T(1,128)}, /*index=5*/f32[1,512]{1,0:T(1,128)}) custom-call(bf16[256,512]{1,0:T(8,128)(2,1)S(1)} %get-tuple-element.18.refs_0_, bf16[256,512]{1,0:T(8,128)(2,1)S(1)} %get-tuple-element.19.refs_1_, ...), custom_call_target="tpu_custom_call" | custom-call | tf_op jit(solution)/shard_map/pallas_call | solution.py:530

commit v6 on v5

--- a/solution.py
+++ b/solution.py
@@ -375,9 +375,6 @@
 
     chunk_to_y(1)
 
-    wait(others(recv_c), recv_sems.at[4])
-    out_ref[...] = dot_nn(p_t[...], recv_c[...].reshape(REGIONS * CAP, WIDTH)).astype(BF)
-
 
     chunk_to_y(2)
     wait(others(gs1), recv_sems.at[6])
@@ -409,6 +406,9 @@
     wait(others(gs2), recv_sems.at[8])
     gs3[zz] = jnp.sum(gs2[...], axis=0)
     along_z(gs3, 5)
+
+    wait(others(recv_c), recv_sems.at[4])
+    out_ref[...] = dot_nn(p_t[...], recv_c[...].reshape(REGIONS * CAP, WIDTH)).astype(BF)
 
     wait(others(recv_d), recv_sems.at[7])
     grad_n = dot_nn(p_t[...], recv_d[...].reshape(REGIONS * CAP, WIDTH))

time: 66.6 us -> 66.6 us (level)
  no operation moved by 1% of the time
where the time goes in v6:
time: 66.6 us; the launch traced here: 66.4 us
  Pallas kernels  65.8 us (99%)
    pallas_call x1, Pallas kernels, on_device(): pl.pallas_call(kernel, out_shape=shapes, in_specs=[hbm] * 9, out_specs=[v...  64.9 us

profile of v6, /device:TPU:1, one launch (start us, length us, event | category | flops | bytes accessed | tf_op | source)
XLA Modules:
  0.0 66.4 jit_solution(6732046486601133534)
XLA Ops:
  0.6 64.9 %shard_map.136 = (bf16[256,512]{1,0:T(8,128)(2,1)S(1)}, bf16[256,512]{1,0:T(8,128)(2,1)S(1)}, f32[48,64]{1,0:T(8,128)S(1)}, f32[16,64]{1,0:T(8,128)S(1)}, f32[1,512]{1,0:T(1,128)S(1)}, /*index=5*/f32[1,512]{1,0:T(1,128)S(1)}) custom-call(bf16[256,512]{1,0:T(8,128)(2,1)} %bitcast.11, s32[1,256]{1,0:T(1,128)} %rs_hbm.1, s32[1,256]{1,0:T(1,128)} %ps_hbm.1, ...), custom_call_target="tpu_custom_call" | custom-call | tf_op jit(solution)/shard_map/pallas_call | solution.py:520
  65.6 0.9 %shard_map.137 = (bf16[256,512]{1,0:T(8,128)(2,1)}, bf16[256,512]{1,0:T(8,128)(2,1)}, f32[48,64]{1,0:T(8,128)}, f32[16,64]{1,0:T(8,128)}, f32[1,512]{1,0:T(1,128)}, /*index=5*/f32[1,512]{1,0:T(1,128)}) custom-call(bf16[256,512]{1,0:T(8,128)(2,1)S(1)} %get-tuple-element.18.refs_0_, bf16[256,512]{1,0:T(8,128)(2,1)S(1)} %get-tuple-element.19.refs_1_, ...), custom_call_target="tpu_custom_call" | custom-call | tf_op jit(solution)/shard_map/pallas_call | solution.py:530
